TPU v7x, 512 devices: a whole 4x8x8 slice. The times are simulated.
512 devices in a mesh: seq: 128 (over y, x, z_hi), ch: 4 (over z_lo, core).
Axes of the slice: x: 4, y: 8, z: 8 (z_hi: 4, z_lo: 2; z = z_hi * 2 + z_lo), core: 2. Of those that a mesh axis runs over, the one named last changes fastest.
Arguments:
- dna_features: bfloat16 [2, 8192, 1280], P(None, 'seq'), may hold values from -6 to 6
- gain_a: float32 [1280], replicated, may hold values from 0.25 to 1.75
- conv_a: bfloat16 [5, 1280, 1408], P(None, 'seq', 'ch'), may hold values from -0.078125 to 0.078125
- bias_a: float32 [1408], P('ch'), may hold values from -3 to 3
- gain_b: float32 [1408], replicated, may hold values from 0.25 to 1.75
- conv_b: bfloat16 [5, 1408, 1536], P(None, 'seq', 'ch'), may hold values from -0.0625 to 0.0625
- bias_b: float32 [1536], P('ch'), may hold values from -3 to 3
- grad_out: bfloat16 [2, 2048, 1536], P(None, 'seq', 'ch'), may hold values from -6 to 6
Outputs:
- pooled_out: bfloat16 [2, 2048, 1536], P(None, 'seq', 'ch')
- input_grad: bfloat16 [2, 8192, 1280], P(None, 'seq', 'ch')
All inputs are finite; a program needn't handle non-finite values.
Results may differ from a plain program's by a relative error of at most 0.018.
Values may be sent and summed in bfloat16 or wider, within the bound.
A program may use at most 128 MiB of HBM per device.

v0:
```python
import math

import jax
import jax.numpy as jnp
from jax import lax
from jax.sharding import PartitionSpec as P

EPS = 1e-06
ROOT = math.sqrt(2.0 / math.pi)


def with_halo(block, sides, width):
    for axis, dim in sides:
        count = lax.axis_size(axis)
        forward = [(i, i + 1) for i in range(count - 1)]
        backward = [(target, source) for source, target in forward]
        low = lax.ppermute(
            lax.slice_in_dim(block, block.shape[dim] - width, None, axis=dim), axis, forward
        )
        high = lax.ppermute(lax.slice_in_dim(block, 0, width, axis=dim), axis, backward)
        block = jnp.concatenate([low, block, high], axis=dim)
    return block


def gelu_tanh(z):
    return 0.5 * z * (1.0 + jnp.tanh(ROOT * (z + 0.044715 * z * z * z)))


def gelu_slope(z):
    t = jnp.tanh(ROOT * (z + 0.044715 * z * z * z))
    return 0.5 * (1.0 + t) + 0.5 * z * (1.0 - t * t) * ROOT * (1.0 + 3.0 * 0.044715 * z * z)


def pool_pairs(v):
    return v.reshape(v.shape[0], v.shape[1] // 2, 2, v.shape[2]).sum(axis=2) * 0.5


def repeat_half(v):
    return (jnp.repeat(v.astype(jnp.float32), 2, axis=1) * 0.5).astype(jnp.bfloat16)


def conv_rows(padded, weight, length):
    total = jnp.einsum(
        "wtc,co->wto", padded[:, 0:length], weight[0], preferred_element_type=jnp.float32
    )
    for offset in range(1, weight.shape[0]):
        total = total + jnp.einsum(
            "wtc,co->wto",
            padded[:, offset : offset + length],
            weight[offset],
            preferred_element_type=jnp.float32,
        )
    return total


def conv_back(padded, weight, length):
    total = jnp.einsum(
        "wto,co->wtc", padded[:, 4 : 4 + length], weight[0], preferred_element_type=jnp.float32
    )
    for offset in range(1, weight.shape[0]):
        start = 4 - offset
        total = total + jnp.einsum(
            "wto,co->wtc",
            padded[:, start : start + length],
            weight[offset],
            preferred_element_type=jnp.float32,
        )
    return total


def per_device(dna_features, gain_a, conv_a, bias_a, gain_b, conv_b, bias_b, grad_out):
    rows_in = dna_features.shape[1]
    rows_mid = rows_in // 2
    width_in = dna_features.shape[2]
    width_mid = gain_b.shape[0]
    share_mid = bias_a.shape[0]
    share_in = width_in // lax.axis_size("ch")
    ch_index = lax.axis_index("ch")
    whole_a, whole_b = (
        lax.all_gather(conv_a, "seq", axis=1, tiled=True),
        lax.all_gather(conv_b, "seq", axis=1, tiled=True),
    )
    feat = dna_features.astype(jnp.float32)
    scale_a = lax.rsqrt(jnp.mean(feat * feat, axis=-1, keepdims=True) + EPS)
    act_a = gelu_tanh(feat * scale_a * gain_a).astype(jnp.bfloat16)
    padded_a = with_halo(act_a, (("seq", 1),), 2)
    conv_out_a = conv_rows(padded_a, whole_a, rows_in)
    mid = pool_pairs(conv_out_a + bias_a).astype(jnp.bfloat16)
    gain_part = lax.dynamic_slice_in_dim(gain_b, ch_index * share_mid, share_mid, 0)
    mid_f = mid.astype(jnp.float32)
    squares = lax.psum(jnp.sum(mid_f * mid_f, axis=-1, keepdims=True), "ch")
    scale_b = lax.rsqrt(squares / width_mid + EPS)
    act_part = gelu_tanh(mid_f * scale_b * gain_part).astype(jnp.bfloat16)
    act_full = lax.all_gather(act_part, "ch", axis=2, tiled=True)
    padded_b = with_halo(act_full, (("seq", 1),), 2)
    conv_out_b = conv_rows(padded_b, whole_b, rows_mid)
    pooled_out = pool_pairs(conv_out_b + bias_b).astype(jnp.bfloat16)
    grad_b = repeat_half(grad_out)
    grad_pad_b = with_halo(grad_b, (("seq", 1),), 2)
    partial_b = conv_back(grad_pad_b, whole_b, rows_mid)
    back_share = lax.psum_scatter(
        partial_b.astype(jnp.bfloat16), "ch", scatter_dimension=2, tiled=True
    ).astype(jnp.float32)
    normed_b = mid_f * scale_b
    grad_n = back_share * gelu_slope(normed_b * gain_part) * gain_part
    inner_b = lax.psum(jnp.sum(grad_n * normed_b, axis=-1, keepdims=True), "ch") / width_mid
    grad_mid = (scale_b * (grad_n - normed_b * inner_b)).astype(jnp.bfloat16)
    grad_a = repeat_half(grad_mid)
    grad_pad_a = with_halo(grad_a, (("seq", 1),), 2)
    partial_a = conv_back(grad_pad_a, whole_a, rows_in)
    back_share_a = lax.psum_scatter(
        partial_a.astype(jnp.bfloat16), "ch", scatter_dimension=2, tiled=True
    ).astype(jnp.float32)
    feat_part = lax.dynamic_slice_in_dim(feat, ch_index * share_in, share_in, 2)
    gain_part_a = lax.dynamic_slice_in_dim(gain_a, ch_index * share_in, share_in, 0)
    normed_a = feat_part * scale_a
    grad_na = back_share_a * gelu_slope(normed_a * gain_part_a) * gain_part_a
    inner_a = lax.psum(jnp.sum(grad_na * normed_a, axis=-1, keepdims=True), "ch") / width_in
    input_grad = (scale_a * (grad_na - normed_a * inner_a)).astype(jnp.bfloat16)
    return (pooled_out, input_grad)


def solution(mesh):
    in_specs = (
        P(None, "seq", None),
        P(),
        P(None, "seq", "ch"),
        P("ch"),
        P(),
        P(None, "seq", "ch"),
        P("ch"),
        P(None, "seq", "ch"),
    )
    out_specs = (P(None, "seq", "ch"), P(None, "seq", "ch"))
    return jax.shard_map(
        per_device, mesh=mesh, in_specs=in_specs, out_specs=out_specs, check_vma=False
    )
```

profile of v0, /device:TPU:1, one launch (start us, length us, event | category | flops | bytes accessed | tf_op | source)
XLA Modules:
  0.0 461.8 jit_solution(9902586635221733371)
XLA Ops:
  7.2 1.5 copy.30
  8.8 1.5 copy.39
  10.3 1.1 multiply_reduce_fusion
  11.4 1.3 fusion.32
  12.8 6.6 %collective-permute-start = (bf16[2,2,1280]{2,1,0:T(2,128)(2,1)S(1)}, bf16[2,2,1280]{2,1,0:T(2,128)(2,1)S(1)}, u32[]{:S(2)}, u32[]{:S(2)}) collective-permute-start(bf16[2,2,1280]{2,1,0:T(2,128)(2,1)S(1)} %get-tuple-element.14), channel_id=1, source_target_pairs={{0,4},{4,8},{8,12},{12,16},{16,20},{20,24},{24,28},{28,32},{32,36}... | collective-permute-start | bytes 30728 | tf_op jit(solution)/shard_map/ppermute | solution.py:17
  19.4 1.3 collective-permute-start.1
  20.7 0.7 multiply_convert_fusion.3
  21.6 1.3 collective-permute-start.4
  22.9 8.3 %collective-permute-start.5 = (bf16[2,2,384]{2,1,0:T(2,128)(2,1)S(1)}, bf16[2,2,384]{2,1,0:T(2,128)(2,1)S(1)}, u32[]{:S(2)}, u32[]{:S(2)}) collective-permute-start(bf16[2,2,384]{2,1,0:T(2,128)(2,1)S(1)} %get-tuple-element.23), channel_id=1, source_target_pairs={{0,4},{4,8},{8,12},{12,16},{16,20},{20,24},{24,28},{28,32},{32,36}... | collective-permute-start | bytes 9224 | tf_op jit(solution)/shard_map/ppermute | solution.py:17
  31.2 1.9 convert_element_type.60
  33.0 0.8 dynamic_slice.11
  33.8 0.8 dynamic_slice.9
  34.6 135.1 %all-gather.3.cloned.1.call-done = bf16[5,1280,352]{2,0,1:T(8,128)(2,1)} async-done(((bf16[5,10,352]{2,0,1:T(8,128)(2,1)}), bf16[5,1280,352]{2,0,1:T(8,128)(2,1)}) %all-gather.3.cloned.1.call-update) | async-done | bytes 4505616 | tf_op jit(solution)/shard_map/all_gather | solution.py:80
  169.7 24.0 %fusion.101 = (bf16[1,1280,352]{2,0,1:T(2,128)(2,1)}, bf16[1,1280,352]{2,0,1:T(2,128)(2,1)}, bf16[1,1280,352]{2,0,1:T(2,128)(2,1)}, bf16[1,1280,352]{2,0,1:T(2,128)(2,1)}, bf16[1,1280,352]{2,0,1:T(2,128)(2,1)}) fusion(bf16[5,1280,352]{2,0,1:T(8,128)(2,1)} %all-gather.3.cloned.1.call-done), kind=kLoop, calls=%fused_computation.149 | loop fusion | bytes 9011200 | tf_op jit(solution)/shard_map/slice | solution.py:50
  193.7 4.0 copy.53
  197.6 0.4 fusion.24
  198.1 4.9 %copy.54 = bf16[1,1280,352]{1,2,0:T(8,128)(2,1)} copy(bf16[1,1280,352]{2,0,1:T(2,128)(2,1)} %get-tuple-element.10) | data formatting | bytes 1802240
  203.0 4.0 copy.52
  206.9 4.0 copy.56
  210.9 4.9 %copy.55 = bf16[1,1280,352]{1,2,0:T(8,128)(2,1)} copy(bf16[1,1280,352]{2,0,1:T(2,128)(2,1)} %get-tuple-element.9) | data formatting | bytes 1802240
  215.8 0.4 fusion.14
  216.3 1.6 fusion.20
  217.9 0.4 fusion.8
  218.3 0.4 fusion.7
  219.2 108.7 %all-gather.5.cloned.1.call-done = bf16[5,1408,384]{2,0,1:T(8,128)(2,1)} async-done(((bf16[5,11,384]{2,0,1:T(8,128)(2,1)}), bf16[5,1408,384]{2,0,1:T(8,128)(2,1)}) %all-gather.5.cloned.1.call-update) | async-done | bytes 5406736 | tf_op jit(solution)/shard_map/all_gather | solution.py:81
  327.8 23.2 %fusion.100 = (bf16[1,1408,384]{2,0,1:T(2,128)(2,1)S(1)}, bf16[1,1408,384]{2,0,1:T(2,128)(2,1)S(1)}, bf16[1,1408,384]{2,0,1:T(2,128)(2,1)S(1)}, bf16[1,1408,384]{2,0,1:T(2,128)(2,1)S(1)}, bf16[1,1408,384]{2,0,1:T(2,128)(2,1)S(1)}) fusion(bf16[5,1408,384]{2,0,1:T(8,128)(2,1)} %all-gather.5.cloned.1.call-done), kind=kLoop, calls=%fused_computation.148 | loop fusion | bytes 10813440 | tf_op jit(solution)/shard_map/slice | solution.py:50
  351.1 0.5 fusion.35
  351.6 0.5 fusion.33
  352.0 0.5 fusion.4
  352.5 0.5 fusion.37
  353.1 0.7 copy-done.2
  353.8 0.7 copy-done.5
  354.4 0.7 copy-done.6
  355.2 1.1 fusion.5
  356.3 2.3 copy.48
  358.6 1.1 reshape.45
  359.9 6.8 %psum.21 = f32[2,32,1]{1,0,2:T(2,128)S(1)} all-reduce(f32[2,32,1]{1,0,2:T(2,128)S(1)} %bitcast.76), channel_id=1, replica_groups=mesh['seq'=128,'ch'=4] {'ch'}, use_global_device_ids=true, to_apply=%region_3.0 | all-reduce | flops 64 | bytes 512 | tf_op jit(solution)/shard_map/psum | solution.py:91
  366.7 13.2 %reduce-scatter.7.cloned.1.call-done = bf16[352,64]{1,0:T(8,128)(2,1)} async-done(((bf16[1408,64]{1,0:T(8,128)(2,1)}), bf16[352,64]{1,0:T(8,128)(2,1)}) %reduce-scatter.7.cloned.1.call-update) | async-done | bytes 45072
  379.9 1.0 reshape.46
  381.3 5.2 %psum.22 = f32[2,32,1]{1,0,2:T(2,128)S(1)} all-reduce(f32[2,32,1]{1,0,2:T(2,128)S(1)} %bitcast.77), channel_id=1, replica_groups=mesh['seq'=128,'ch'=4] {'ch'}, use_global_device_ids=true, to_apply=%region_7.0 | all-reduce | flops 64 | bytes 512 | tf_op jit(solution)/shard_map/psum | solution.py:106
  386.8 2.4 fusion.18
  389.2 0.8 copy.36
  390.0 9.4 %all_gather.10 = bf16[2,32,1408]{1,0,2:T(2,128)(2,1)S(1)} all-gather(bf16[2,32,352]{1,0,2:T(2,128)(2,1)} %copy.36), channel_id=1, replica_groups=mesh['seq'=128,'ch'=4] {'ch'}, dimensions={2}, use_global_device_ids=true | all-gather | bytes 225280 | tf_op jit(solution)/shard_map/all_gather | solution.py:94
  399.4 1.6 copy.37
  401.1 0.9 fusion.103
  402.0 2.7 fusion.36
  404.6 1.3 collective-permute-start.6
  405.9 5.0 %collective-permute-start.7 = (bf16[2,2,352]{2,1,0:T(2,128)(2,1)S(1)}, bf16[2,2,352]{2,1,0:T(2,128)(2,1)S(1)}, u32[]{:S(2)}, u32[]{:S(2)}) collective-permute-start(bf16[2,2,352]{2,1,0:T(2,128)(2,1)S(1)} %get-tuple-element.19), channel_id=1, source_target_pairs={{0,4},{4,8},{8,12},{12,16},{16,20},{20,24},{24,28},{28,32},{32,36}... | collective-permute-start | bytes 8456 | tf_op jit(solution)/shard_map/ppermute | solution.py:17
  410.9 5.5 %collective-permute-start.2 = (bf16[2,2,1408]{2,1,0:T(2,128)(2,1)S(1)}, bf16[2,2,1408]{2,1,0:T(2,128)(2,1)S(1)}, u32[]{:S(2)}, u32[]{:S(2)}) collective-permute-start(bf16[2,2,1408]{2,1,0:T(2,128)(2,1)S(1)} %get-tuple-element.16), channel_id=1, source_target_pairs={{0,4},{4,8},{8,12},{12,16},{16,20},{20,24},{24,28},{28,32},{32,36}... | collective-permute-start | bytes 33800 | tf_op jit(solution)/shard_map/ppermute | solution.py:17
  416.4 1.3 collective-permute-start.3
  417.7 0.3 fusion.22
  418.0 0.3 fusion
  418.4 0.3 fusion.12
  418.7 0.5 copy-done.8
  419.2 0.3 fusion.2
  419.6 0.5 copy.50
  420.1 1.1 reshape.47
  421.2 2.1 fusion.34
  423.3 1.9 fusion.11
  426.1 0.6 multiply_convert_fusion.4
  426.7 21.0 %reduce-scatter.9.cloned.1.call-done = bf16[320,128]{1,0:T(8,128)(2,1)} async-done(((bf16[1280,128]{1,0:T(8,128)(2,1)}), bf16[320,128]{1,0:T(8,128)(2,1)}) %reduce-scatter.9.cloned.1.call-update) | async-done | bytes 81936
  447.7 1.0 reshape.48
  449.2 5.2 %psum.23 = f32[2,64,1]{1,0,2:T(2,128)S(1)} all-reduce(f32[2,64,1]{1,0,2:T(2,128)S(1)} %bitcast.78), channel_id=1, replica_groups=mesh['seq'=128,'ch'=4] {'ch'}, use_global_device_ids=true, to_apply=%region_10.0 | all-reduce | flops 128 | bytes 1024 | tf_op jit(solution)/shard_map/psum | solution.py:118
  454.4 0.9 multiply_convert_fusion
  (69 shorter events, 2.9 us)
Async XLA Ops:
  7.2 162.5 %all-gather.3.cloned.1.call-start = ((), (), s32[]{:S(2)}) async-start(), calls=%async_computation.2 | async-start | bytes 7925760 | tf_op jit(solution)/shard_map/all_gather | solution.py:80
  8.7 319.1 %all-gather.5.cloned.1.call-start = ((), (), s32[]{:S(2)}) async-start(), calls=%async_computation.3 | async-start | bytes 8718336 | tf_op jit(solution)/shard_map/all_gather | solution.py:81
  10.3 369.6 %reduce-scatter.7.cloned.1.call-start = ((), (), s32[]{:S(2)}) async-start(), calls=%async_computation.4 | async-start | bytes 450560
  12.8 184.8 %collective-permute-start = (bf16[2,2,1280]{2,1,0:T(2,128)(2,1)S(1)}, bf16[2,2,1280]{2,1,0:T(2,128)(2,1)S(1)}, u32[]{:S(2)}, u32[]{:S(2)}) collective-permute-start(bf16[2,2,1280]{2,1,0:T(2,128)(2,1)S(1)} %get-tuple-element.14), channel_id=1, source_target_pairs={{0,4},{4,8},{8,12},{12,16},{16,20},{20,24},{24,28},{28,32},{32,36}... | collective-permute-start | bytes 30728 | tf_op jit(solution)/shard_map/ppermute | solution.py:17
  19.4 196.4 %collective-permute-start.1 = (bf16[2,2,1280]{2,1,0:T(2,128)(2,1)S(1)}, bf16[2,2,1280]{2,1,0:T(2,128)(2,1)S(1)}, u32[]{:S(2)}, u32[]{:S(2)}) collective-permute-start(bf16[2,2,1280]{2,1,0:T(2,128)(2,1)S(1)} %get-tuple-element.15), channel_id=1, source_target_pairs={{4,0},{8,4},{12,8},{16,12},{20,16},{24,20},{28,24},{32,28},{36,32}... | collective-permute-start | bytes 30728 | tf_op jit(solution)/shard_map/ppermute | solution.py:20
  21.6 13.0 %collective-permute-start.4 = (bf16[2,2,384]{2,1,0:T(2,128)(2,1)S(1)}, bf16[2,2,384]{2,1,0:T(2,128)(2,1)S(1)}, u32[]{:S(2)}, u32[]{:S(2)}) collective-permute-start(bf16[2,2,384]{2,1,0:T(2,128)(2,1)S(1)} %get-tuple-element.22), channel_id=1, source_target_pairs={{4,0},{8,4},{12,8},{16,12},{20,16},{24,20},{28,24},{32,28},{36,32}... | collective-permute-start | bytes 9224 | tf_op jit(solution)/shard_map/ppermute | solution.py:20
  22.9 329.7 %collective-permute-start.5 = (bf16[2,2,384]{2,1,0:T(2,128)(2,1)S(1)}, bf16[2,2,384]{2,1,0:T(2,128)(2,1)S(1)}, u32[]{:S(2)}, u32[]{:S(2)}) collective-permute-start(bf16[2,2,384]{2,1,0:T(2,128)(2,1)S(1)} %get-tuple-element.23), channel_id=1, source_target_pairs={{0,4},{4,8},{8,12},{12,16},{16,20},{20,24},{24,28},{28,32},{32,36}... | collective-permute-start | bytes 9224 | tf_op jit(solution)/shard_map/ppermute | solution.py:17
  215.8 2.5 copy-start.7
  215.8 2.5 copy-start.12
  351.1 1.5 copy-start
  351.1 2.0 copy-start.4
  351.1 2.7 copy-start.2
  351.1 3.3 copy-start.5
  351.1 4.1 copy-start.6
  359.7 88.0 %reduce-scatter.9.cloned.1.call-start = ((), (), s32[]{:S(2)}) async-start(), calls=%async_computation.5 | async-start | bytes 409600
  401.1 17.0 %copy-start.9 = (f32[2,64,1280]{2,1,0:T(8,128)S(1)}, f32[2,64,1280]{2,1,0:T(8,128)}, u32[]{:S(2)}) copy-start(f32[2,64,1280]{2,1,0:T(8,128)} %fusion.18) | copy-start | bytes 1966084
  404.6 13.1 %collective-permute-start.6 = (bf16[2,2,352]{2,1,0:T(2,128)(2,1)S(1)}, bf16[2,2,352]{2,1,0:T(2,128)(2,1)S(1)}, u32[]{:S(2)}, u32[]{:S(2)}) collective-permute-start(bf16[2,2,352]{2,1,0:T(2,128)(2,1)S(1)} %get-tuple-element.18), channel_id=1, source_target_pairs={{4,0},{8,4},{12,8},{16,12},{20,16},{24,20},{28,24},{32,28},{36,32}... | collective-permute-start | bytes 8456 | tf_op jit(solution)/shard_map/ppermute | solution.py:20
  405.9 12.5 %collective-permute-start.7 = (bf16[2,2,352]{2,1,0:T(2,128)(2,1)S(1)}, bf16[2,2,352]{2,1,0:T(2,128)(2,1)S(1)}, u32[]{:S(2)}, u32[]{:S(2)}) collective-permute-start(bf16[2,2,352]{2,1,0:T(2,128)(2,1)S(1)} %get-tuple-element.19), channel_id=1, source_target_pairs={{0,4},{4,8},{8,12},{12,16},{16,20},{20,24},{24,28},{28,32},{32,36}... | collective-permute-start | bytes 8456 | tf_op jit(solution)/shard_map/ppermute | solution.py:17
  410.9 10.3 %collective-permute-start.2 = (bf16[2,2,1408]{2,1,0:T(2,128)(2,1)S(1)}, bf16[2,2,1408]{2,1,0:T(2,128)(2,1)S(1)}, u32[]{:S(2)}, u32[]{:S(2)}) collective-permute-start(bf16[2,2,1408]{2,1,0:T(2,128)(2,1)S(1)} %get-tuple-element.16), channel_id=1, source_target_pairs={{0,4},{4,8},{8,12},{12,16},{16,20},{20,24},{24,28},{28,32},{32,36}... | collective-permute-start | bytes 33800 | tf_op jit(solution)/shard_map/ppermute | solution.py:17
  416.4 8.8 %collective-permute-start.3 = (bf16[2,2,1408]{2,1,0:T(2,128)(2,1)S(1)}, bf16[2,2,1408]{2,1,0:T(2,128)(2,1)S(1)}, u32[]{:S(2)}, u32[]{:S(2)}) collective-permute-start(bf16[2,2,1408]{2,1,0:T(2,128)(2,1)S(1)} %get-tuple-element.17), channel_id=1, source_target_pairs={{4,0},{8,4},{12,8},{16,12},{20,16},{24,20},{28,24},{32,28},{36,32}... | collective-permute-start | bytes 33800 | tf_op jit(solution)/shard_map/ppermute | solution.py:20
  418.0 1.2 copy-start.8
  419.2 2.0 copy-start.11
  419.6 3.7 copy-start.14
  420.1 5.1 %copy-start.1 = (bf16[1,1408,384]{2,0,1:T(2,128)(2,1)S(1)}, bf16[1,1408,384]{2,0,1:T(2,128)(2,1)}, u32[]{:S(2)}) copy-start(bf16[1,1408,384]{2,0,1:T(2,128)(2,1)} %copy-done) | copy-start | bytes 3244036
  421.2 4.4 copy-start.3
  421.2 4.4 copy-start.13
  425.2 23.7 %copy-start.10 = (f32[2,64,1280]{2,1,0:T(8,128)S(1)}, f32[2,64,1280]{2,1,0:T(8,128)}, u32[]{:S(2)}) copy-start(f32[2,64,1280]{2,1,0:T(8,128)} %convert_element_type.60) | copy-start | bytes 1966084
Sparse Core Ops, SparseCore 0:
  12.4 157.1 all-gather.2
  174.7 153.0 all-gather.4
  359.8 20.0 reduce-scatter.6
  421.3 26.3 reduce-scatter.8
where the time goes:
time: 463 us; the launch traced here: 462 us
  waiting for transfers between devices  278 us (60%)
  local copies, waits for them, and re-layouts  87.1 us (19%)
  starting transfers between devices  30.7 us (7%)
  blocking collectives  26.5 us (6%)
  matrix products  17.3 us (4%)
  between operations  14.3 us (3%)
  other arithmetic  7.78 us (2%)
    all_gather x1, waiting for transfers between devices, per_device(): lax.all_gather(conv_a, 'seq', axis=1, tiled=True)  135 us
    all_gather x1, waiting for transfers between devices, per_device(): lax.all_gather(conv_b, 'seq', axis=1, tiled=True)  109 us
    slice x2, local copies, waits for them, and re-layouts, conv_rows(): weight[offset]  47.2 us
    unnamed x47, local copies, waits for them, and re-layouts  34.5 us
    unnamed x6, waiting for transfers between devices  34.3 us
    ppermute x4, starting transfers between devices, with_halo(): lax.ppermute(lax.slice_in_dim(block, block.shape[dim] - width, None, axis...  25.3 us
    all_gather x1, blocking collectives, per_device(): act_full = lax.all_gather(act_part, 'ch', axis=2, tiled=True)  9.41 us
  transfers between devices with their start and end apart: 12, of which 4 were waited for; matrix products, arithmetic and copies ran while one was open for 20% of the time, Pallas kernels for 0%

commit v1 on v0

v1 whole, which is shorter than its diff:
```python
import math

import jax
import jax.numpy as jnp
import numpy as np
from jax import lax
from jax.experimental import pallas as pl
from jax.experimental.pallas import tpu as pltpu
from jax.sharding import PartitionSpec as P

EPS = 1e-06
ROOT = math.sqrt(2.0 / math.pi)
MESH = pl.DeviceIdType.MESH
BF = jnp.bfloat16
F32 = jnp.float32
NY, NX, NZ, NC = 8, 4, 4, 4
CIN, CMID = 1280, 1408
EDGE = 16
WIDE = 2048
TAPS = 5 * 384


def gelu_tanh(z):
    return 0.5 * z * (1.0 + jnp.tanh(ROOT * (z + 0.044715 * z * z * z)))


def gelu_slope(z):
    t = jnp.tanh(ROOT * (z + 0.044715 * z * z * z))
    return 0.5 * (1.0 + t) + 0.5 * z * (1.0 - t * t) * ROOT * (1.0 + 3.0 * 0.044715 * z * z)


def index_tables():
    lanes = np.full((8, 1536), -100000, np.int32)
    rows = np.full((512, 8), -100000, np.int32)
    for zb in range(NZ):
        for xb in range(NX):
            for yb in range(NY):
                for i in range(10):
                    lanes[0, zb * 384 + xb * 80 + yb * 10 + i] = ((yb * 4 + xb) * 4 + zb) * 10 + i
            for yy in range(2):
                for i in range(11):
                    q = yy * 48 + xb * 11 + i
                    here = ((yy * 4 + xb) * 4 + zb) * 11 + i
                    lanes[1, zb * 128 + q] = here
                    rows[zb * 128 + q, 3] = here
                for i in range(10):
                    q = xb * 20 + yy * 10 + i
                    here = ((yy * 4 + xb) * 4 + zb) * 10 + i
                    lanes[3, zb * 128 + q] = here
                    rows[zb * 128 + q, 4] = here
    for cb in range(NC):
        for xb in range(NX):
            for yy in range(2):
                for i in range(11):
                    lanes[2, cb * 128 + yy * 48 + xb * 11 + i] = (((cb * 2 + yy) * 4 + xb) * 4) * 11 + i
                for i in range(10):
                    rows[cb * 128 + xb * 20 + yy * 10 + i, 0] = xb * 80 + (cb * 2 + yy) * 10 + i
    for k in range(5):
        for yb in range(NY):
            for i in range(10):
                rows[k * 80 + yb * 10 + i, 1] = yb * 64 + k * 10 + i
        for xb in range(NX):
            for i in range(11):
                rows[k * 48 + xb * 11 + i, 2] = xb * 64 + k * 11 + i
    return lanes, rows


def dot(a, b):
    return lax.dot_general(a, b, (((1,), (0,)), ((), ())), preferred_element_type=F32)


def dot_t(a, b):
    return lax.dot_general(a, b, (((1,), (1,)), ((), ())), preferred_element_type=F32)


def one_hot_lanes(table, depth):
    row = lax.broadcasted_iota(jnp.int32, (depth, table.shape[1]), 0)
    return jnp.where(row == table, 1.0, 0.0).astype(BF)


def one_hot_rows(table, depth):
    col = lax.broadcasted_iota(jnp.int32, (table.shape[0], depth), 1)
    return jnp.where(col == table, 1.0, 0.0).astype(BF)


def three_parts(v):
    high = v.astype(BF).astype(F32)
    rest = v - high
    middle = rest.astype(BF).astype(F32)
    return high, middle, rest - middle


def spread_gain(gain, hot):
    high, middle, low = three_parts(gain)
    row = lax.broadcasted_iota(jnp.int32, (16, gain.shape[1]), 0)
    stack = jnp.where(row == 0, high, jnp.where(row == 1, middle, jnp.where(row == 2, low, 0.0)))
    return jnp.sum(dot(stack.astype(BF), hot), axis=0, keepdims=True)


def kernel(
    feat_ref, wa_ref, wb_ref, gain_a_ref, bias_a_ref, gain_b_ref, bias_b_ref, g_ref, lanes_ref, rows_ref,
    pooled_ref, grad_ref,
    first_a, first_b, whole_a, turned_a, whole_b, bias_pad,
    act_slot, act_prev, act_next, act_rows, taps_a, send_act,
    g_slot, g_prev, g_next, g_rows,
    back_rows, back_send, back_recv,
    acc_a, mid_send, mid_recv,
    x_send, x_recv, b_slot, b_prev, b_next, b_rows,
    pool_send, pool_recv, acc_b,
    in_send, in_recv, gm_slot, gm_prev, gm_next, gm_rows,
    out_rows, out_send, out_recv, ia_send, ia_recv,
    s_fa, r_fa, s_fb, r_fb, s_wb, r_wb, s_wa, r_wa, s_col, r_col, s_edge, r_edge,
    s_b, r_b, s_x, r_x, s_o, r_o,
):
    seq = lax.axis_index("seq")
    ch = lax.axis_index("ch")
    zh = seq % NZ
    col = seq // NZ
    xi = col % NX
    yi = col // NX
    own = zh * NC + ch
    pending = []

    def start(src, dst, ssem, rsem, dev):
        copy = pltpu.make_async_remote_copy(
            src_ref=src, dst_ref=dst, send_sem=ssem, recv_sem=rsem, device_id=dev, device_id_type=MESH
        )
        copy.start()
        pending.append(copy)

    def arrived(dst, ssem, rsem):
        pltpu.make_async_remote_copy(
            src_ref=dst, dst_ref=dst, send_sem=ssem, recv_sem=rsem, device_id=(seq, ch), device_id_type=MESH
        ).wait_recv()

    def at_y(d):
        return ((((yi + d + NY) % NY) * NX + xi) * NZ + zh, ch)

    def at_x(d):
        return ((yi * NX + (xi + d + NX) % NX) * NZ + zh, ch)

    def at_z(d):
        return (col * NZ + (zh + d) % NZ, ch)

    def at_c(d):
        return (seq, (ch + d) % NC)

    def at_col(d):
        return (((col + d + 32) % 32) * NZ + zh, ch)

    def member(d):
        t = (own + d) % 16
        return t, (col * NZ + t // NC, t % NC)

    barrier = pltpu.get_barrier_semaphore()

    def greet(dev):
        pl.semaphore_signal(barrier, inc=1, device_id=dev, device_id_type=MESH)

    for d in (1, 2, 3):
        greet(at_x(d))
    for d in (-1, 1):
        greet(at_y(d))
        greet(at_col(d))

    @pl.loop(1, 16)
    def _(d):
        greet(member(d)[1])

    first_a[yi] = jnp.zeros((64, 384), BF)
    bias_pad[...] = jnp.zeros((8, 384), F32)
    bias_pad[0:1, 0:352] = bias_a_ref[...]
    pack_a = jnp.zeros((64, 352), F32)
    pack_b = jnp.zeros((64, 384), F32)
    for k in range(5):
        pick = lax.broadcasted_iota(jnp.int32, (64, 10), 0) == lax.broadcasted_iota(jnp.int32, (64, 10), 1) + 10 * k
        pack_a += dot(jnp.where(pick, 1.0, 0.0).astype(BF), wa_ref[k])
        pick = lax.broadcasted_iota(jnp.int32, (64, 11), 0) == lax.broadcasted_iota(jnp.int32, (64, 11), 1) + 11 * k
        pack_b += dot(jnp.where(pick, 1.0, 0.0).astype(BF), wb_ref[k])
    first_a[yi, :, 0:352] = pack_a.astype(BF)
    first_b[xi] = pack_b.astype(BF)
    whole_a[320:512, :] = jnp.zeros((192, WIDE), BF)
    whole_a[0:320, TAPS:WIDE] = jnp.zeros((320, WIDE - TAPS), BF)
    whole_b[:, TAPS:WIDE] = jnp.zeros((512, WIDE - TAPS), BF)
    for c in range(NC):
        whole_b[c * 128 + 96 : c * 128 + 128, 0:TAPS] = jnp.zeros((32, TAPS), BF)
    taps_a[:, :, 384:512] = jnp.zeros((5, 256, 128), BF)
    pl.semaphore_wait(barrier, 22)

    half = ((0, 32), (32, 32))

    def ring_fa(r, way):
        sign = 1 if way == 0 else -1
        at, n = (0, 64) if r < 3 else half[way]
        b = (yi - sign * r + NY) % NY
        ref = first_a.at[b, pl.ds(at, n), :]
        start(ref, ref, s_fa.at[way, r], r_fa.at[way, r], at_y(sign))

    def ring_fa_done(r, way):
        sign = 1 if way == 0 else -1
        at, n = (0, 64) if r < 3 else half[way]
        b = (yi - sign * (r + 1) + NY) % NY
        arrived(first_a.at[b, pl.ds(at, n), :], s_fa.at[way, r], r_fa.at[way, r])

    for way in (0, 1):
        ring_fa(0, way)
    for d in (1, 2, 3):
        start(first_b.at[xi], first_b.at[xi], s_fb.at[d], r_fb.at[d], at_x(d))

    g_slot[zh] = g_ref[...]
    for d in (1, 2, 3):
        start(g_ref, g_slot.at[zh], s_col.at[0, d], r_col.at[0, d], at_z(d))

    feat = feat_ref[...].astype(F32)
    inv_a = lax.rsqrt(jnp.sum(feat * feat, axis=-1, keepdims=True) * (1.0 / CIN) + EPS)
    act = gelu_tanh(feat * inv_a * gain_a_ref[...]).astype(BF)

    def slot_of(d):
        return (zh - d + NZ) % NZ

    for zb in range(NZ):
        hot = one_hot_lanes(lanes_ref[0:1, zb * 384 : (zb + 1) * 384], CIN)
        send_act[zb] = dot(act, hot).astype(BF)
    act_slot[zh] = send_act[zh]
    for d in (1, 2, 3):
        t = (zh + d) % NZ
        start(send_act.at[t], act_slot.at[zh], s_col.at[1, d], r_col.at[1, d], at_z(d))

    for d in (1, 2, 3):
        arrived(first_b.at[(xi - d + NX) % NX], s_fb.at[d], r_fb.at[d])
    hot_b = one_hot_rows(rows_ref[0:240, 2:3], 256)
    block = dot(hot_b, first_b[...].reshape(256, 384)).astype(BF)

    def place_b(b):
        return pl.multiple_of((b // 2) * 128 + (b % 2) * 48, 16)

    for k in range(5):
        whole_b[pl.ds(place_b(yi), 48), k * 384 : (k + 1) * 384] = block[k * 48 : (k + 1) * 48]
    taps_half = ((0, 1152), (1152, 768))

    def ring_wb(r, way):
        sign = 1 if way == 0 else -1
        at, n = (0, TAPS) if r < 3 else taps_half[way]
        ref = whole_b.at[pl.ds(place_b((yi - sign * r + NY) % NY), 48), pl.ds(at, n)]
        start(ref, ref, s_wb.at[way, r], r_wb.at[way, r], at_y(sign))

    def ring_wb_done(r, way):
        sign = 1 if way == 0 else -1
        at, n = (0, TAPS) if r < 3 else taps_half[way]
        ref = whole_b.at[pl.ds(place_b((yi - sign * (r + 1) + NY) % NY), 48), pl.ds(at, n)]
        arrived(ref, s_wb.at[way, r], r_wb.at[way, r])

    def ring_wa(r, way):
        sign = 1 if way == 0 else -1
        at, n = (0, TAPS) if r < 1 else taps_half[way]
        b = (xi - sign * r + NX) % NX
        ref = whole_a.at[pl.ds(pl.multiple_of(b * 80, 16), 80), pl.ds(at, n)]
        start(ref, ref, s_wa.at[way, r], r_wa.at[way, r], at_x(sign))

    def ring_wa_done(r, way):
        sign = 1 if way == 0 else -1
        at, n = (0, TAPS) if r < 1 else taps_half[way]
        b = (xi - sign * (r + 1) + NX) % NX
        ref = whole_a.at[pl.ds(pl.multiple_of(b * 80, 16), 80), pl.ds(at, n)]
        arrived(ref, s_wa.at[way, r], r_wa.at[way, r])

    for way in (0, 1):
        ring_wb(0, way)
    for r in range(3):
        for way in (0, 1):
            ring_fa_done(r, way)
            ring_fa(r + 1, way)
    for way in (0, 1):
        ring_fa_done(3, way)
    hot_a = one_hot_rows(rows_ref[0:400, 1:2], 512)
    block = dot(hot_a, first_a[...].reshape(512, 384)).astype(BF)
    for k in range(5):
        whole_a[pl.ds(pl.multiple_of(xi * 80, 16), 80), k * 384 : (k + 1) * 384] = block[k * 80 : (k + 1) * 80]
    for way in (0, 1):
        ring_wa(0, way)
    for way in (0, 1):
        ring_wb_done(0, way)
        ring_wb(1, way)

    def edges(slots, rows, prev, nxt, n):
        for w in range(2):
            lo = slots.at[0, pl.ds(w * rows, EDGE), :]
            hi = slots.at[3, pl.ds(w * rows + rows - EDGE, EDGE), :]
            start(hi, prev.at[w], s_edge.at[n, w], r_edge.at[n, w], at_col(1))
            start(lo, nxt.at[w], s_edge.at[n, 2 + w], r_edge.at[n, 2 + w], at_col(-1))

    def edges_done(prev, nxt, n):
        for w in range(2):
            arrived(prev.at[w], s_edge.at[n, w], r_edge.at[n, w])
            arrived(nxt.at[w], s_edge.at[n, 2 + w], r_edge.at[n, 2 + w])

    is_first = jnp.where(col == 0, 0.0, 1.0).astype(F32)
    is_last = jnp.where(col == 31, 0.0, 1.0).astype(F32)

    def lay(slots, rows, prev, nxt, where):
        tiles = where.shape[1]
        for w in range(2):
            for t in range(tiles):
                lanes = slice(t * 128, (t + 1) * 128)
                where[w, t, 0:EDGE, :] = prev[w, :, lanes].astype(F32) * is_first
                for z in range(NZ):
                    at = EDGE + z * rows
                    where[w, t, at : at + rows, :] = slots[z, w * rows : (w + 1) * rows, lanes].astype(F32)
                at = EDGE + NZ * rows
                where[w, t, at : at + EDGE, :] = nxt[w, :, lanes].astype(F32) * is_last

    def pooled_taps(where, rows):
        tiles = where.shape[1]
        parts = [[[where[w, t, pl.ds(EDGE + d, rows, stride=2), :] for t in range(tiles)] for w in range(2)]
                 for d in range(-2, 4)]
        out = []
        for k in range(5):
            wins = []
            for w in range(2):
                wins.append(jnp.concatenate(
                    [((parts[k][w][t] + parts[k + 1][w][t]) * 0.5).astype(BF) for t in range(tiles)], axis=1))
            out.append(jnp.concatenate(wins, axis=0))
        return out

    def shifted(where, rows):
        tiles = where.shape[1]
        return [
            jnp.concatenate([
                jnp.concatenate([where[w, t, EDGE + d : EDGE + d + rows, :].astype(BF) for t in range(tiles)], axis=1)
                for w in range(2)], axis=0)
            for d in (-1, 0, 1)
        ]

    def back_conv(before, here, after, weight, rows, where):
        none = jnp.zeros((2 * rows, WIDE - TAPS), BF)
        even = jnp.concatenate([after, here, here, before, before, none], axis=1)
        odd = jnp.concatenate([after, after, here, here, before, none], axis=1)
        total = dot_t(jnp.concatenate([even, odd], axis=0), weight[...]) * 0.5
        even, odd = total[0 : 2 * rows], total[2 * rows : 4 * rows]
        for w in range(2):
            for t in range(where.shape[1]):
                lanes = slice(t * 128, (t + 1) * 128)
                where[w, t, pl.ds(0, rows, stride=2), :] = even[w * rows : (w + 1) * rows, lanes]
                where[w, t, pl.ds(1, rows, stride=2), :] = odd[w * rows : (w + 1) * rows, lanes]

    for d in (1, 2, 3):
        arrived(g_slot.at[slot_of(d)], s_col.at[0, d], r_col.at[0, d])
    edges(g_slot, 16, g_prev, g_next, 0)
    for d in (1, 2, 3):
        arrived(act_slot.at[slot_of(d)], s_col.at[1, d], r_col.at[1, d])
    edges(act_slot, 64, act_prev, act_next, 1)

    gain_b = jnp.concatenate([gain_b_ref[...], jnp.zeros((1, 128), F32)], axis=1)
    hot = one_hot_lanes(lanes_ref[2:3, 0:512] + zh * 11, CMID + 128)
    gain_b_all = spread_gain(gain_b, hot)
    hot = one_hot_lanes(lanes_ref[1:2, 0:512] + ch * 352, CMID + 128)
    gain_b_own = spread_gain(gain_b, hot)
    hot = one_hot_lanes(lanes_ref[3:4, 0:512] + ch * 320, CIN)
    gain_a_own = spread_gain(gain_a_ref[...], hot)
    feat_own = dot(feat_ref[...], hot)
    normed_a = feat_own * inv_a
    factor_a = gelu_slope(normed_a * gain_a_own) * gain_a_own

    for way in (0, 1):
        ring_wb_done(1, way)
        ring_wb(2, way)
    for way in (0, 1):
        ring_wa_done(0, way)
        ring_wa(1, way)
    edges_done(act_prev, act_next, 1)
    lay(act_slot, 64, act_prev, act_next, act_rows)
    for k, tap in enumerate(pooled_taps(act_rows, 128)):
        taps_a[k, :, 0:384] = tap
    for way in (0, 1):
        ring_wb_done(2, way)
        ring_wb(3, way)
    edges_done(g_prev, g_next, 0)
    lay(g_slot, 16, g_prev, g_next, g_rows)
    for way in (0, 1):
        ring_wa_done(1, way)

    total = dot(taps_a[0], whole_a[:, 0:384])
    for k in range(1, 5):
        total += dot(taps_a[k], whole_a[:, k * 384 : (k + 1) * 384])
    for w in range(2):
        acc_a[w] = total[w * 128 : (w + 1) * 128]
    for z in range(NZ):
        for w in range(2):
            mid_send[z, w * 32 : (w + 1) * 32, :] = total[w * 128 + z * 32 : w * 128 + (z + 1) * 32].astype(BF)
    for d in (1, 2, 3):
        t = (zh + d) % NZ
        start(mid_send.at[t], mid_recv.at[zh], s_col.at[2, d], r_col.at[2, d], at_z(d))

    for way in (0, 1):
        ring_wb_done(3, way)
    before, here, after = shifted(g_rows, 64)
    back_conv(before, here, after, whole_b, 64, back_rows)
    for z in range(NZ):
        for c in range(NC):
            for w in range(2):
                back_send[z * NC + c, w * 32 : (w + 1) * 32, :] = back_rows[w, c, z * 32 : (z + 1) * 32, :].astype(BF)

    def scatter(src, dst, ssem, rsem, whole):
        @pl.loop(1, 16)
        def _(d):
            t, dev = member(d)
            pltpu.make_async_remote_copy(
                src_ref=src.at[t] if whole else src.at[t // NC], dst_ref=dst.at[own], send_sem=ssem.at[d],
                recv_sem=rsem.at[d], device_id=dev, device_id_type=MESH,
            ).start()

    def scattered(dst, ssem, rsem):
        @pl.loop(1, 16)
        def _(d):
            arrived(dst.at[(own - d + 16) % 16], ssem.at[d], rsem.at[d])

    def scatter_sent(src, ssem, rsem):
        @pl.loop(1, 16)
        def _(d):
            pltpu.make_async_remote_copy(
                src_ref=src.at[0], dst_ref=src.at[0], send_sem=ssem.at[d], recv_sem=rsem.at[d],
                device_id=(seq, ch), device_id_type=MESH,
            ).wait_send()

    scatter(back_send, back_recv, s_b, r_b, True)
    back_recv[own] = back_send[own]

    for d in (1, 2, 3):
        arrived(mid_recv.at[slot_of(d)], s_col.at[2, d], r_col.at[2, d])
    total = jnp.concatenate([acc_a[w, pl.ds(pl.multiple_of(zh * 32, 32), 32), :] for w in range(2)], axis=0)
    for d in (1, 2, 3):
        total += mid_recv[slot_of(d)].astype(F32)
    mid = (total + bias_pad[0:1, :]).astype(BF)
    mid_f = mid.astype(F32)
    squares = jnp.sum(mid_f * mid_f, axis=-1, keepdims=True)
    mid_wide = jnp.concatenate([mid, jnp.zeros((64, 128), BF)], axis=1)
    mid_own = dot(mid_wide, one_hot_lanes(lanes_ref[1:2, 0:512], 512))
    lane = lax.broadcasted_iota(jnp.int32, (64, 128), 1)
    high, middle, low = three_parts(squares)
    for z in range(NZ):
        piece = mid_own[:, z * 128 : (z + 1) * 128]
        piece = jnp.where(lane == 96, high, jnp.where(lane == 97, middle, jnp.where(lane == 98, low, piece)))
        x_send[z] = piece.astype(BF)
    scatter(x_send, x_recv, s_x, r_x, False)
    x_recv[own] = x_send[zh]

    hot = one_hot_rows(rows_ref[:, 0:1], 512)
    for k in range(4):
        turned_a[:, k * 512 : (k + 1) * 512] = dot(hot, whole_a[:, k * 512 : (k + 1) * 512]).astype(BF)

    def inverse(z):
        total = jnp.zeros((64, 1), F32)
        for c in range(NC):
            part = x_recv[z * NC + c, :, 96:99].astype(F32)
            total += jnp.sum(part, axis=-1, keepdims=True)
        return lax.rsqrt(total * (1.0 / CMID) + EPS)

    scattered(x_recv, s_x, r_x)
    inv_b = inverse(zh)
    normed_b = mid_own * inv_b
    factor_b = gelu_slope(normed_b * gain_b_own) * gain_b_own
    scattered(back_recv, s_b, r_b)
    back = jnp.concatenate(
        [
            back_recv[z * NC].astype(F32) + back_recv[z * NC + 1].astype(F32)
            + back_recv[z * NC + 2].astype(F32) + back_recv[z * NC + 3].astype(F32)
            for z in range(NZ)
        ],
        axis=1,
    )
    grad_n = back * factor_b
    in_send[...] = jnp.broadcast_to(jnp.sum(grad_n * normed_b, axis=-1, keepdims=True), (64, 128))
    for d in (1, 2, 3):
        start(in_send, in_recv.at[ch], s_col.at[3, d], r_col.at[3, d], at_c(d))

    for z in range(NZ):
        inv = inverse(z)
        values = jnp.concatenate([x_recv[z * NC + c].astype(F32) for c in range(NC)], axis=1)
        b_slot[z] = gelu_tanh(values * inv * gain_b_all).astype(BF)
    edges(b_slot, 32, b_prev, b_next, 2)

    inner = in_send[...]
    for d in (1, 2, 3):
        at = (ch - d + NC) % NC
        arrived(in_recv.at[at], s_col.at[3, d], r_col.at[3, d])
        inner += in_recv[at]
    inner = jnp.concatenate([inner * (1.0 / CMID)] * 4, axis=1)
    grad_mid = (inv_b * (grad_n - normed_b * inner)).astype(BF)
    gm_slot[zh] = dot(grad_mid, one_hot_rows(rows_ref[:, 3:4], 384)).astype(BF)
    for d in (1, 2, 3):
        start(gm_slot.at[zh], gm_slot.at[zh], s_col.at[4, d], r_col.at[4, d], at_z(d))

    edges_done(b_prev, b_next, 2)
    lay(b_slot, 32, b_prev, b_next, b_rows)
    taps = pooled_taps(b_rows, 64)
    total = dot(taps[0], whole_b[:, 0:384])
    for k in range(1, 5):
        total += dot(taps[k], whole_b[:, k * 384 : (k + 1) * 384])
    for w in range(2):
        acc_b[w] = total[w * 64 : (w + 1) * 64]
    for z in range(NZ):
        for w in range(2):
            pool_send[z, w * 16 : (w + 1) * 16, :] = total[w * 64 + z * 16 : w * 64 + (z + 1) * 16].astype(BF)

    for d in (1, 2, 3):
        arrived(gm_slot.at[slot_of(d)], s_col.at[4, d], r_col.at[4, d])
    edges(gm_slot, 32, gm_prev, gm_next, 3)
    for d in (1, 2, 3):
        t = (zh + d) % NZ
        start(pool_send.at[t], pool_recv.at[zh], s_col.at[5, d], r_col.at[5, d], at_z(d))

    edges_done(gm_prev, gm_next, 3)
    lay(gm_slot, 32, gm_prev, gm_next, gm_rows)
    before, here, after = shifted(gm_rows, 128)
    back_conv(before, here, after, turned_a, 128, out_rows)
    for z in range(NZ):
        for c in range(NC):
            for w in range(2):
                out_send[z * NC + c, w * 64 : (w + 1) * 64, :] = out_rows[w, c, z * 64 : (z + 1) * 64, :].astype(BF)
    scatter(out_send, out_recv, s_o, r_o, True)
    out_recv[own] = out_send[own]

    for d in (1, 2, 3):
        arrived(pool_recv.at[slot_of(d)], s_col.at[5, d], r_col.at[5, d])
    total = jnp.concatenate([acc_b[w, pl.ds(pl.multiple_of(zh * 16, 16), 16), :] for w in range(2)], axis=0)
    for d in (1, 2, 3):
        total += pool_recv[slot_of(d)].astype(F32)
    pooled_ref[...] = (total + bias_b_ref[...]).astype(BF)

    scattered(out_recv, s_o, r_o)
    back = jnp.concatenate(
        [
            out_recv[z * NC].astype(F32) + out_recv[z * NC + 1].astype(F32)
            + out_recv[z * NC + 2].astype(F32) + out_recv[z * NC + 3].astype(F32)
            for z in range(NZ)
        ],
        axis=1,
    )
    grad_n = back * factor_a
    ia_send[...] = jnp.broadcast_to(jnp.sum(grad_n * normed_a, axis=-1, keepdims=True), (128, 128))
    for d in (1, 2, 3):
        start(ia_send, ia_recv.at[ch], s_col.at[6, d], r_col.at[6, d], at_c(d))
    hot = one_hot_rows(rows_ref[:, 4:5], 384)
    inner = ia_send[...]
    for d in (1, 2, 3):
        at = (ch - d + NC) % NC
        arrived(ia_recv.at[at], s_col.at[6, d], r_col.at[6, d])
        inner += ia_recv[at]
    inner = jnp.concatenate([inner * (1.0 / CIN)] * 4, axis=1)
    grad = (inv_a * (grad_n - normed_a * inner)).astype(BF)
    grad_ref[...] = dot(grad, hot)[:, 0:320].astype(BF)

    for copy in pending:
        copy.wait_send()
    scatter_sent(back_send, s_b, r_b)
    scatter_sent(x_send, s_x, r_x)
    scatter_sent(out_send, s_o, r_o)


def per_device(dna_features, gain_a, conv_a, bias_a, gain_b, conv_b, bias_b, grad_out):
    lanes, rows = index_tables()
    dma = pltpu.SemaphoreType.DMA
    vmem = pltpu.VMEM
    pooled, grad = pl.pallas_call(
        kernel,
        out_shape=(jax.ShapeDtypeStruct((32, 384), BF), jax.ShapeDtypeStruct((128, 320), BF)),
        in_specs=[pl.BlockSpec(memory_space=vmem)] * 10,
        out_specs=[pl.BlockSpec(memory_space=vmem)] * 2,
        scratch_shapes=[
            vmem((8, 64, 384), BF), vmem((4, 64, 384), BF), vmem((512, WIDE), BF), vmem((512, WIDE), BF),
            vmem((512, WIDE), BF), vmem((8, 384), F32),
            vmem((4, 128, 384), BF), vmem((2, 16, 384), BF), vmem((2, 16, 384), BF), vmem((2, 3, 288, 128), F32),
            vmem((5, 256, 512), BF), vmem((4, 128, 384), BF),
            vmem((4, 32, 384), BF), vmem((2, 16, 384), BF), vmem((2, 16, 384), BF), vmem((2, 3, 96, 128), F32),
            vmem((2, 4, 128, 128), F32), vmem((16, 64, 128), BF), vmem((16, 64, 128), BF),
            vmem((2, 128, 384), F32), vmem((4, 64, 384), BF), vmem((4, 64, 384), BF),
            vmem((4, 64, 128), BF), vmem((16, 64, 128), BF), vmem((4, 64, 512), BF), vmem((2, 16, 512), BF),
            vmem((2, 16, 512), BF), vmem((2, 4, 160, 128), F32),
            vmem((4, 32, 384), BF), vmem((4, 32, 384), BF), vmem((2, 64, 384), F32),
            vmem((64, 128), F32), vmem((4, 64, 128), F32), vmem((4, 64, 384), BF), vmem((2, 16, 384), BF),
            vmem((2, 16, 384), BF), vmem((2, 3, 160, 128), F32),
            vmem((2, 4, 256, 128), F32), vmem((16, 128, 128), BF), vmem((16, 128, 128), BF),
            vmem((128, 128), F32), vmem((4, 128, 128), F32),
            dma((2, 4)), dma((2, 4)), dma((4,)), dma((4,)), dma((2, 4)), dma((2, 4)), dma((2, 2)), dma((2, 2)),
            dma((7, 4)), dma((7, 4)), dma((4, 4)), dma((4, 4)),
            dma((16,)), dma((16,)), dma((16,)), dma((16,)), dma((16,)), dma((16,)),
        ],
        compiler_params=pltpu.CompilerParams(
            collective_id=0, has_side_effects=True, vmem_limit_bytes=48 * 1024 * 1024
        ),
        cost_estimate=pl.CostEstimate(flops=3_000_000_000, bytes_accessed=8_000_000, transcendentals=800_000),
    )(
        dna_features.reshape(128, CIN), conv_a, conv_b, gain_a.reshape(1, CIN), bias_a.reshape(1, 352),
        gain_b.reshape(1, CMID), bias_b.reshape(1, 384), grad_out.reshape(32, 384), jnp.asarray(lanes), jnp.asarray(rows),
    )
    return pooled.reshape(2, 16, 384), grad.reshape(2, 64, 320)


def solution(mesh):
    return jax.shard_map(
        per_device,
        mesh=mesh,
        in_specs=(
            P(None, "seq", None), P(), P(None, "seq", "ch"), P("ch"), P(), P(None, "seq", "ch"), P("ch"),
            P(None, "seq", "ch"),
        ),
        out_specs=(P(None, "seq", "ch"), P(None, "seq", "ch")),
        check_vma=False,
    )
```

time: 463 us -> 109 us (0.24)
  waiting for transfers between devices: 278 us -> 0 us
  Pallas kernels: 0 us -> 99.3 us
  local copies, waits for them, and re-layouts: 87.1 us -> 8.4 us
  starting transfers between devices: 30.7 us -> 0 us
  blocking collectives: 26.5 us -> 0 us
  matrix products: 17.3 us -> 0 us
  between operations: 14.3 us -> 0.66 us
  other arithmetic: 7.78 us -> 0 us
    all_gather x2 -> x0, waiting for transfers between devices: 244 us -> none  [the longest x1 135 us: per_device(): lax.all_gather(conv_a, 'seq', axis=1, tiled=True)]
    pallas_call x0 -> x1, Pallas kernels: none -> 99.3 us  [per_device(): pl.pallas_call(kernel, out_shape=(jax.ShapeDtypeStruct((32, 384), BF), ja...]
    slice x6 -> x0, local copies, waits for them, and re-layouts: 48.2 us -> none  [the longest x2 47.2 us: conv_rows(): weight[offset]]
    unnamed x6 -> x0, waiting for transfers between devices: 34.3 us -> none
    ppermute x8 -> x0, starting transfers between devices: 30.5 us -> none  [the longest x4 25.3 us: with_halo(): lax.ppermute(lax.slice_in_dim(block, block.shape[dim] - width, None, axis...]
    unnamed x47 -> x14, local copies, waits for them, and re-layouts: 34.5 us -> 5.63 us
    dot_general x20 -> x0, matrix products: 17.3 us -> none  [the longest x8 8.25 us: conv_rows(): jnp.einsum('wtc,co->wto', padded[:, offset:offset + length], weight[offse...]
    psum x3 -> x0, blocking collectives: 17.1 us -> none  [the longest x1 6.79 us: per_device(): squares = lax.psum(jnp.sum(mid_f * mid_f, axis=-1, keepdims=True), 'ch')]
  transfers between devices with their start and end apart: 12 -> 0, of which waited for: 4 -> 0; matrix products, arithmetic and copies ran while one was open for 20% -> 0% of each run, Pallas kernels for 0% -> 0%
where the time goes in v1:
time: 109 us; the launch traced here: 108 us
  Pallas kernels  99.3 us (91%)
  local copies, waits for them, and re-layouts  8.4 us (8%)
    pallas_call x1, Pallas kernels, per_device(): pl.pallas_call(kernel, out_shape=(jax.ShapeDtypeStruct((32, 384), BF), ja...  99.3 us
    unnamed x14, local copies, waits for them, and re-layouts  5.63 us

profile of v1, /device:TPU:1, one launch (start us, length us, event | category | flops | bytes accessed | tf_op | source)
XLA Modules:
  0.0 108.3 jit_solution(17174617471615173295)
XLA Ops:
  0.6 0.0 copy-start.3
  0.6 0.7 reshape.30.bias_a_ref
  1.3 0.7 reshape.32.bias_b_ref
  2.0 0.7 reshape.29.gain_a_ref
  2.7 0.7 reshape.31.gain_b_ref
  3.4 0.0 copy-done.3
  3.4 0.0 copy-start
  3.4 1.0 copy-done
  4.4 0.0 copy-start.1
  4.4 0.8 copy-done.1
  5.2 0.0 copy-start.2
  5.2 0.8 copy-done.2
  6.0 0.0 copy-start.4
  6.1 0.9 copy-done.4
  7.0 0.0 copy-start.5
  7.0 0.8 copy-done.5
  7.8 99.3 %shard_map.113 = (bf16[32,384]{1,0:T(8,128)(2,1)S(1)}, bf16[128,320]{1,0:T(8,128)(2,1)S(1)}) custom-call(bf16[128,1280]{1,0:T(8,128)(2,1)S(1)} %bitcast.6, bf16[5,10,352]{2,1,0:T(8,128)(2,1)S(1)} %copy-done.1, bf16[5,11,384]{2,1,0:T(8,128)(2,1)S(1)} %copy-done.2, f32[1,1280]{1,0:T(1,128)S(1)} %reshape.29.gain_a_ref, f32[1,352]{1,0:T(1,128)S(1)} %reshape.30.bias_a_ref, ...), custom_call_target="tpu_custom_call" | custom-call | flops 3000000000 | bytes 8000000 | tf_op jit(solution)/shard_map/pallas_call | solution.py:564
  107.1 0.6 copy.14
  107.7 0.6 copy.15
Async XLA Ops:
  0.6 2.8 %copy-start.3 = (bf16[2,16,384]{2,1,0:T(8,128)(2,1)S(1)}, bf16[2,16,384]{2,1,0:T(8,128)(2,1)}, u32[]{:S(2)}) copy-start(bf16[2,16,384]{2,1,0:T(8,128)(2,1)} %param.17) | copy-start | bytes 73732
  3.4 1.0 copy-start
  4.4 0.8 copy-start.1
  5.2 0.8 copy-start.2
  6.0 0.9 copy-start.4
  7.0 0.8 copy-start.5

commit v2 on v1

--- a/solution.py
+++ b/solution.py
@@ -98,19 +98,20 @@
 
 
 def kernel(
+    feat_in, wa_in, wb_in, gain_a_in, bias_a_in, gain_b_in, bias_b_in, g_in, lanes_in, rows_in,
+    pooled_ref, grad_ref,
     feat_ref, wa_ref, wb_ref, gain_a_ref, bias_a_ref, gain_b_ref, bias_b_ref, g_ref, lanes_ref, rows_ref,
-    pooled_ref, grad_ref,
     first_a, first_b, whole_a, turned_a, whole_b, bias_pad,
     act_slot, act_prev, act_next, act_rows, taps_a, send_act,
-    g_slot, g_prev, g_next, g_rows,
-    back_rows, back_send, back_recv,
+    g_slot, g_send, g_prev, g_next, g_rows,
+    back_rows, back_over, back_twin, back_send, back_recv,
     acc_a, mid_send, mid_recv,
     x_send, x_recv, b_slot, b_prev, b_next, b_rows,
     pool_send, pool_recv, acc_b,
     in_send, in_recv, gm_slot, gm_prev, gm_next, gm_rows,
-    out_rows, out_send, out_recv, ia_send, ia_recv,
+    out_rows, out_over, out_twin, out_send, out_recv, ia_send, ia_recv,
     s_fa, r_fa, s_fb, r_fb, s_wb, r_wb, s_wa, r_wa, s_col, r_col, s_edge, r_edge,
-    s_b, r_b, s_x, r_x, s_o, r_o,
+    s_b, r_b, s_x, r_x, s_o, r_o, s_in, s_gm, s_edge_gm, s_af, r_af, s_tw, r_tw,
 ):
     seq = lax.axis_index("seq")
     ch = lax.axis_index("ch")
@@ -119,7 +120,21 @@
     xi = col % NX
     yi = col // NX
     own = zh * NC + ch
+    core = ch % 2
+    zl = ch // 2
+    twin = (seq, ch + 1 - 2 * core)
+    own8 = zh * 2 + zl
     pending = []
+    loads = [
+        pltpu.make_async_copy(src, dst, s_in.at[i])
+        for i, (src, dst) in enumerate((
+            (wa_in, wa_ref), (wb_in, wb_ref), (rows_in, rows_ref), (lanes_in, lanes_ref), (feat_in, feat_ref),
+            (gain_a_in, gain_a_ref), (g_in, g_ref), (bias_a_in, bias_a_ref), (gain_b_in, gain_b_ref),
+            (bias_b_in, bias_b_ref),
+        ))
+    ]
+    for load in loads:
+        load.start()
 
     def start(src, dst, ssem, rsem, dev):
         copy = pltpu.make_async_remote_copy(
@@ -149,8 +164,14 @@
         return (((col + d + 32) % 32) * NZ + zh, ch)
 
     def member(d):
-        t = (own + d) % 16
-        return t, (col * NZ + t // NC, t % NC)
+        tz, tc = (zh + d // NC) % NZ, (ch + d % NC) % NC
+        return tz * NC + tc, (col * NZ + tz, tc)
+
+    def source(d):
+        return ((zh - d // NC + NZ) % NZ) * NC + (ch - d % NC + NC) % NC
+
+    def beside(way, z):
+        return (((col + way + 32) % 32) * NZ + z, ch)
 
     barrier = pltpu.get_barrier_semaphore()
 
@@ -161,15 +182,21 @@
         greet(at_x(d))
     for d in (-1, 1):
         greet(at_y(d))
-        greet(at_col(d))
+        for z in range(NZ):
+            greet(beside(d, z))
 
     @pl.loop(1, 16)
     def _(d):
         greet(member(d)[1])
 
+    for load in loads:
+        load.wait()
+    gain_a = gain_a_ref[...].reshape(1, CIN)
+    gain_b = gain_b_ref[...].reshape(1, CMID)
+
     first_a[yi] = jnp.zeros((64, 384), BF)
     bias_pad[...] = jnp.zeros((8, 384), F32)
-    bias_pad[0:1, 0:352] = bias_a_ref[...]
+    bias_pad[0:1, 0:352] = bias_a_ref[...].reshape(1, 352)
     pack_a = jnp.zeros((64, 352), F32)
     pack_b = jnp.zeros((64, 384), F32)
     for k in range(5):
@@ -185,9 +212,10 @@
     for c in range(NC):
         whole_b[c * 128 + 96 : c * 128 + 128, 0:TAPS] = jnp.zeros((32, TAPS), BF)
     taps_a[:, :, 384:512] = jnp.zeros((5, 256, 128), BF)
-    pl.semaphore_wait(barrier, 22)
+    pl.semaphore_wait(barrier, 28)
 
     half = ((0, 32), (32, 32))
+    parts = ((0, 1152), (1152, 768))
 
     def ring_fa(r, way):
         sign = 1 if way == 0 else -1
@@ -202,85 +230,111 @@
         b = (yi - sign * (r + 1) + NY) % NY
         arrived(first_a.at[b, pl.ds(at, n), :], s_fa.at[way, r], r_fa.at[way, r])
 
+    def place_a(b):
+        return pl.multiple_of(b * 80, 16)
+
+    def place_b(b):
+        return pl.multiple_of((b // 2) * 128 + (b % 2) * 48, 16)
+
+    def ring_wb(r, way, c):
+        sign = 1 if way == 0 else -1
+        ref = whole_b.at[pl.ds(place_b((yi - sign * r + NY) % NY), 48), pl.ds(*parts[c])]
+        start(ref, ref, s_wb.at[way, r, c], r_wb.at[way, r, c], at_y(sign))
+
+    def ring_wb_done(r, way, c):
+        sign = 1 if way == 0 else -1
+        ref = whole_b.at[pl.ds(place_b((yi - sign * (r + 1) + NY) % NY), 48), pl.ds(*parts[c])]
+        arrived(ref, s_wb.at[way, r, c], r_wb.at[way, r, c])
+
+    def ring_wa(r, way, c):
+        sign = 1 if way == 0 else -1
+        ref = whole_a.at[pl.ds(place_a((xi - sign * r + NX) % NX), 80), pl.ds(*parts[c])]
+        start(ref, ref, s_wa.at[way, r, c], r_wa.at[way, r, c], at_x(sign))
+
+    def ring_wa_done(r, way, c):
+        sign = 1 if way == 0 else -1
+        ref = whole_a.at[pl.ds(place_a((xi - sign * (r + 1) + NX) % NX), 80), pl.ds(*parts[c])]
+        arrived(ref, s_wa.at[way, r, c], r_wa.at[way, r, c])
+
+    def pass_on(ring, done, r, last, rank):
+        for way in (0, 1):
+            c = way if rank == 0 else 1 - way
+            done(r, way, c)
+            if r + 1 < last or (r + 1 == last and rank == 0):
+                ring(r + 1, way, c)
+
     for way in (0, 1):
         ring_fa(0, way)
     for d in (1, 2, 3):
         start(first_b.at[xi], first_b.at[xi], s_fb.at[d], r_fb.at[d], at_x(d))
 
-    g_slot[zh] = g_ref[...]
-    for d in (1, 2, 3):
-        start(g_ref, g_slot.at[zh], s_col.at[0, d], r_col.at[0, d], at_z(d))
-
-    feat = feat_ref[...].astype(F32)
-    inv_a = lax.rsqrt(jnp.sum(feat * feat, axis=-1, keepdims=True) * (1.0 / CIN) + EPS)
-    act = gelu_tanh(feat * inv_a * gain_a_ref[...]).astype(BF)
-
     def slot_of(d):
         return (zh - d + NZ) % NZ
 
-    for zb in range(NZ):
-        hot = one_hot_lanes(lanes_ref[0:1, zb * 384 : (zb + 1) * 384], CIN)
-        send_act[zb] = dot(act, hot).astype(BF)
-    act_slot[zh] = send_act[zh]
-    for d in (1, 2, 3):
+    def inverse_a(v):
+        return lax.rsqrt(jnp.sum(v * v, axis=-1, keepdims=True) * (1.0 / CIN) + EPS)
+
+    feat = feat_ref[core].astype(F32)
+    act = gelu_tanh(feat * inverse_a(feat) * gain_a).astype(BF)
+    mine = pl.ds(pl.multiple_of(core * 64, 64), 64)
+    others = pl.ds(pl.multiple_of(64 - core * 64, 64), 64)
+
+    def subset(d):
         t = (zh + d) % NZ
-        start(send_act.at[t], act_slot.at[zh], s_col.at[1, d], r_col.at[1, d], at_z(d))
+        hot = one_hot_lanes(lanes_ref[0:1, pl.ds(pl.multiple_of(t * 384, 128), 384)], CIN)
+        part = dot(act, hot).astype(BF)
+        if d == 0:
+            act_slot[zh, mine, :] = part
+            share_act(0)
+        else:
+            send_act[d] = part
+            start(send_act.at[d], act_slot.at[zh, mine, :], s_col.at[1, d], r_col.at[1, d], at_z(d))
+
+    def share_act(d):
+        ref = act_slot.at[slot_of(d), mine, :]
+        start(ref, ref, s_af.at[d], r_af.at[d], twin)
+
+    def fa_on(r):
+        for way in (0, 1):
+            ring_fa_done(r, way)
+            ring_fa(r + 1, way)
+
+    subset(2)
 
     for d in (1, 2, 3):
         arrived(first_b.at[(xi - d + NX) % NX], s_fb.at[d], r_fb.at[d])
     hot_b = one_hot_rows(rows_ref[0:240, 2:3], 256)
     block = dot(hot_b, first_b[...].reshape(256, 384)).astype(BF)
-
-    def place_b(b):
-        return pl.multiple_of((b // 2) * 128 + (b % 2) * 48, 16)
-
     for k in range(5):
         whole_b[pl.ds(place_b(yi), 48), k * 384 : (k + 1) * 384] = block[k * 48 : (k + 1) * 48]
-    taps_half = ((0, 1152), (1152, 768))
-
-    def ring_wb(r, way):
-        sign = 1 if way == 0 else -1
-        at, n = (0, TAPS) if r < 3 else taps_half[way]
-        ref = whole_b.at[pl.ds(place_b((yi - sign * r + NY) % NY), 48), pl.ds(at, n)]
-        start(ref, ref, s_wb.at[way, r], r_wb.at[way, r], at_y(sign))
-
-    def ring_wb_done(r, way):
-        sign = 1 if way == 0 else -1
-        at, n = (0, TAPS) if r < 3 else taps_half[way]
-        ref = whole_b.at[pl.ds(place_b((yi - sign * (r + 1) + NY) % NY), 48), pl.ds(at, n)]
-        arrived(ref, s_wb.at[way, r], r_wb.at[way, r])
-
-    def ring_wa(r, way):
-        sign = 1 if way == 0 else -1
-        at, n = (0, TAPS) if r < 1 else taps_half[way]
-        b = (xi - sign * r + NX) % NX
-        ref = whole_a.at[pl.ds(pl.multiple_of(b * 80, 16), 80), pl.ds(at, n)]
-        start(ref, ref, s_wa.at[way, r], r_wa.at[way, r], at_x(sign))
-
-    def ring_wa_done(r, way):
-        sign = 1 if way == 0 else -1
-        at, n = (0, TAPS) if r < 1 else taps_half[way]
-        b = (xi - sign * (r + 1) + NX) % NX
-        ref = whole_a.at[pl.ds(pl.multiple_of(b * 80, 16), 80), pl.ds(at, n)]
-        arrived(ref, s_wa.at[way, r], r_wa.at[way, r])
-
-    for way in (0, 1):
-        ring_wb(0, way)
-    for r in range(3):
+    for rank in (0, 1):
         for way in (0, 1):
-            ring_fa_done(r, way)
-            ring_fa(r + 1, way)
+            ring_wb(0, way, way if rank == 0 else 1 - way)
+    fa_on(0)
+    subset(1)
+    fa_on(1)
+    subset(3)
+    fa_on(2)
+    subset(0)
+    g_own = g_ref[...].reshape(32, 384)
+    g_slot[zh] = g_own
+    g_send[...] = g_own
+    for d in (1, 2, 3):
+        start(g_send, g_slot.at[zh], s_col.at[0, d], r_col.at[0, d], at_z(d))
+    hot_a = one_hot_rows(rows_ref[0:400, 1:2], 512)
     for way in (0, 1):
         ring_fa_done(3, way)
-    hot_a = one_hot_rows(rows_ref[0:400, 1:2], 512)
     block = dot(hot_a, first_a[...].reshape(512, 384)).astype(BF)
     for k in range(5):
-        whole_a[pl.ds(pl.multiple_of(xi * 80, 16), 80), k * 384 : (k + 1) * 384] = block[k * 80 : (k + 1) * 80]
-    for way in (0, 1):
-        ring_wa(0, way)
-    for way in (0, 1):
-        ring_wb_done(0, way)
-        ring_wb(1, way)
+        whole_a[pl.ds(place_a(xi), 80), k * 384 : (k + 1) * 384] = block[k * 80 : (k + 1) * 80]
+    for rank in (0, 1):
+        for way in (0, 1):
+            ring_wa(0, way, way if rank == 0 else 1 - way)
+    pass_on(ring_wb, ring_wb_done, 0, 3, 0)
+    for d in (1, 3, 2):
+        arrived(act_slot.at[slot_of(d), mine, :], s_col.at[1, d], r_col.at[1, d])
+        share_act(d)
+    pass_on(ring_wb, ring_wb_done, 0, 3, 1)
 
     def edges(slots, rows, prev, nxt, n):
         for w in range(2):
@@ -343,41 +397,37 @@
                 where[w, t, pl.ds(0, rows, stride=2), :] = even[w * rows : (w + 1) * rows, lanes]
                 where[w, t, pl.ds(1, rows, stride=2), :] = odd[w * rows : (w + 1) * rows, lanes]
 
+    gain_b = jnp.concatenate([gain_b, jnp.zeros((1, 128), F32)], axis=1)
+    hot = one_hot_lanes(lanes_ref[2:3, 0:512] + zh * 11, CMID + 128)
+    gain_b_all = spread_gain(gain_b, hot)
+    pass_on(ring_wb, ring_wb_done, 1, 3, 0)
+    pass_on(ring_wa, ring_wa_done, 0, 1, 0)
+    hot = one_hot_lanes(lanes_ref[1:2, 0:512] + ch * 352, CMID + 128)
+    gain_b_own = spread_gain(gain_b, hot)
     for d in (1, 2, 3):
         arrived(g_slot.at[slot_of(d)], s_col.at[0, d], r_col.at[0, d])
     edges(g_slot, 16, g_prev, g_next, 0)
-    for d in (1, 2, 3):
-        arrived(act_slot.at[slot_of(d)], s_col.at[1, d], r_col.at[1, d])
+    pass_on(ring_wb, ring_wb_done, 1, 3, 1)
+    for d in range(NZ):
+        arrived(act_slot.at[slot_of(d), others, :], s_af.at[d], r_af.at[d])
     edges(act_slot, 64, act_prev, act_next, 1)
-
-    gain_b = jnp.concatenate([gain_b_ref[...], jnp.zeros((1, 128), F32)], axis=1)
-    hot = one_hot_lanes(lanes_ref[2:3, 0:512] + zh * 11, CMID + 128)
-    gain_b_all = spread_gain(gain_b, hot)
-    hot = one_hot_lanes(lanes_ref[1:2, 0:512] + ch * 352, CMID + 128)
-    gain_b_own = spread_gain(gain_b, hot)
     hot = one_hot_lanes(lanes_ref[3:4, 0:512] + ch * 320, CIN)
-    gain_a_own = spread_gain(gain_a_ref[...], hot)
-    feat_own = dot(feat_ref[...], hot)
+    gain_a_own = spread_gain(gain_a, hot)
+    feat_bf = feat_ref[...].reshape(128, CIN)
+    inv_a = inverse_a(feat_bf.astype(F32))
+    feat_own = dot(feat_bf, hot)
+    pass_on(ring_wb, ring_wb_done, 2, 3, 0)
     normed_a = feat_own * inv_a
     factor_a = gelu_slope(normed_a * gain_a_own) * gain_a_own
-
-    for way in (0, 1):
-        ring_wb_done(1, way)
-        ring_wb(2, way)
-    for way in (0, 1):
-        ring_wa_done(0, way)
-        ring_wa(1, way)
+    edges_done(g_prev, g_next, 0)
+    lay(g_slot, 16, g_prev, g_next, g_rows)
     edges_done(act_prev, act_next, 1)
     lay(act_slot, 64, act_prev, act_next, act_rows)
     for k, tap in enumerate(pooled_taps(act_rows, 128)):
         taps_a[k, :, 0:384] = tap
+    pass_on(ring_wa, ring_wa_done, 0, 1, 1)
     for way in (0, 1):
-        ring_wb_done(2, way)
-        ring_wb(3, way)
-    edges_done(g_prev, g_next, 0)
-    lay(g_slot, 16, g_prev, g_next, g_rows)
-    for way in (0, 1):
-        ring_wa_done(1, way)
+        ring_wa_done(1, way, way)
 
     total = dot(taps_a[0], whole_a[:, 0:384])
     for k in range(1, 5):
@@ -391,39 +441,68 @@
         t = (zh + d) % NZ
         start(mid_send.at[t], mid_recv.at[zh], s_col.at[2, d], r_col.at[2, d], at_z(d))
 
+    pass_on(ring_wb, ring_wb_done, 2, 3, 1)
     for way in (0, 1):
-        ring_wb_done(3, way)
+        ring_wb_done(3, way, way)
     before, here, after = shifted(g_rows, 64)
     back_conv(before, here, after, whole_b, 64, back_rows)
-    for z in range(NZ):
-        for c in range(NC):
-            for w in range(2):
-                back_send[z * NC + c, w * 32 : (w + 1) * 32, :] = back_rows[w, c, z * 32 : (z + 1) * 32, :].astype(BF)
-
-    def scatter(src, dst, ssem, rsem, whole):
-        @pl.loop(1, 16)
+    def to_twin(where, per, send, recv, n):
+        for z in range(NZ):
+            for b in range(2):
+                for w in range(2):
+                    piece = where[w, b * 2 + 1 - core, z * per : (z + 1) * per, :]
+                    send[z * 2 + b, w * per : (w + 1) * per, :] = piece.astype(BF)
+        start(send, recv, s_tw.at[n], r_tw.at[n], twin)
+
+    def from_twin(where, per, recv, send, n):
+        arrived(recv, s_tw.at[n], r_tw.at[n])
+        for z in range(NZ):
+            for b in range(2):
+                for w in range(2):
+                    piece = where[w, b * 2 + core, z * per : (z + 1) * per, :]
+                    rows = slice(w * per, (w + 1) * per)
+                    send[z * 2 + b, rows, :] = (piece + recv[z * 2 + b, rows, :].astype(F32)).astype(BF)
+
+    def scatter(src, dst, ssem, rsem):
+        @pl.loop(1, 8)
         def _(d):
-            t, dev = member(d)
+            tz, tb = (zh + d // 2) % NZ, (zl + d % 2) % 2
             pltpu.make_async_remote_copy(
-                src_ref=src.at[t] if whole else src.at[t // NC], dst_ref=dst.at[own], send_sem=ssem.at[d],
-                recv_sem=rsem.at[d], device_id=dev, device_id_type=MESH,
+                src_ref=src.at[tz * 2 + tb], dst_ref=dst.at[own8], send_sem=ssem.at[d], recv_sem=rsem.at[d],
+                device_id=(col * NZ + tz, tb * 2 + core), device_id_type=MESH,
             ).start()
 
+        dst[own8] = src[own8]
+
     def scattered(dst, ssem, rsem):
-        @pl.loop(1, 16)
+        @pl.loop(1, 8)
         def _(d):
-            arrived(dst.at[(own - d + 16) % 16], ssem.at[d], rsem.at[d])
+            arrived(dst.at[((zh - d // 2 + NZ) % NZ) * 2 + (zl - d % 2 + 2) % 2], ssem.at[d], rsem.at[d])
 
     def scatter_sent(src, ssem, rsem):
-        @pl.loop(1, 16)
+        @pl.loop(1, 8)
         def _(d):
             pltpu.make_async_remote_copy(
                 src_ref=src.at[0], dst_ref=src.at[0], send_sem=ssem.at[d], recv_sem=rsem.at[d],
                 device_id=(seq, ch), device_id_type=MESH,
             ).wait_send()
 
-    scatter(back_send, back_recv, s_b, r_b, True)
-    back_recv[own] = back_send[own]
+    def to_row(v):
+        wide = jnp.broadcast_to(v, (v.shape[0], 128))
+        if v.shape[0] < 128:
+            wide = jnp.concatenate([wide, jnp.zeros((128 - v.shape[0], 128), F32)], axis=0)
+        return jnp.transpose(wide)[0:8]
+
+    def to_column(v, rows):
+        return jnp.transpose(jnp.concatenate([v] * 16, axis=0))[0:rows]
+
+    def two_shares(recv):
+        return jnp.concatenate(
+            [recv[z * 2].astype(F32) + recv[z * 2 + 1].astype(F32) for z in range(NZ)], axis=1)
+
+    to_twin(back_rows, 32, back_over, back_twin, 0)
+    from_twin(back_rows, 32, back_twin, back_send, 0)
+    scatter(back_send, back_recv, s_b, r_b)
 
     for d in (1, 2, 3):
         arrived(mid_recv.at[slot_of(d)], s_col.at[2, d], r_col.at[2, d])
@@ -441,8 +520,16 @@
         piece = mid_own[:, z * 128 : (z + 1) * 128]
         piece = jnp.where(lane == 96, high, jnp.where(lane == 97, middle, jnp.where(lane == 98, low, piece)))
         x_send[z] = piece.astype(BF)
-    scatter(x_send, x_recv, s_x, r_x, False)
+    for d in (1, 2, 3):
+        start(x_send.at[zh], x_recv.at[own], s_x.at[d], r_x.at[d], at_c(d))
     x_recv[own] = x_send[zh]
+    far = [(dz, db) for dz in (2, 1, 3) for db in (0, 1)]
+    for n, (dz, db) in enumerate(far):
+        tz, tb = (zh + dz) % NZ, (zl + db) % 2
+        start(x_send.at[tz], x_recv.at[own], s_x.at[4 + n], r_x.at[4 + n], (col * NZ + tz, tb * 2 + core))
+
+    def x_slot(dz, db, side):
+        return x_recv.at[slot_of(dz) * NC + ((zl - db + 2) % 2) * 2 + side]
 
     hot = one_hot_rows(rows_ref[:, 0:1], 512)
     for k in range(4):
@@ -455,40 +542,73 @@
             total += jnp.sum(part, axis=-1, keepdims=True)
         return lax.rsqrt(total * (1.0 / CMID) + EPS)
 
-    scattered(x_recv, s_x, r_x)
+    for d in (1, 2, 3):
+        arrived(x_recv.at[zh * NC + (ch - d + NC) % NC], s_x.at[d], r_x.at[d])
     inv_b = inverse(zh)
     normed_b = mid_own * inv_b
     factor_b = gelu_slope(normed_b * gain_b_own) * gain_b_own
     scattered(back_recv, s_b, r_b)
-    back = jnp.concatenate(
-        [
-            back_recv[z * NC].astype(F32) + back_recv[z * NC + 1].astype(F32)
-            + back_recv[z * NC + 2].astype(F32) + back_recv[z * NC + 3].astype(F32)
-            for z in range(NZ)
-        ],
-        axis=1,
-    )
-    grad_n = back * factor_b
-    in_send[...] = jnp.broadcast_to(jnp.sum(grad_n * normed_b, axis=-1, keepdims=True), (64, 128))
+    grad_n = two_shares(back_recv) * factor_b
+    in_send[...] = to_row(jnp.sum(grad_n * normed_b, axis=-1, keepdims=True))
     for d in (1, 2, 3):
         start(in_send, in_recv.at[ch], s_col.at[3, d], r_col.at[3, d], at_c(d))
 
+    for n, (dz, db) in enumerate(far):
+        arrived(x_slot(dz, db, core), s_x.at[4 + n], r_x.at[4 + n])
+        start(x_slot(dz, db, core), x_slot(dz, db, core), s_x.at[10 + n], r_x.at[10 + n], twin)
+    inner = in_send[...]
+    for d in (1, 2, 3):
+        at = (ch - d + NC) % NC
+        arrived(in_recv.at[at], s_col.at[3, d], r_col.at[3, d])
+        inner += in_recv[at]
+    inner = jnp.concatenate([to_column(inner * (1.0 / CMID), 64)] * 4, axis=1)
+    grad_mid = (inv_b * (grad_n - normed_b * inner)).astype(BF)
+    gm_slot[zh] = dot(grad_mid, one_hot_rows(rows_ref[:, 3:4], 384)).astype(BF)
+    for d in (1, 2, 3):
+        start(gm_slot.at[zh], gm_slot.at[zh], s_col.at[4, d], r_col.at[4, d], at_z(d))
+
+    def last_rows(z, w):
+        return pltpu.make_async_remote_copy(
+            src_ref=gm_slot.at[3, pl.ds(w * 32 + 16, EDGE), :], dst_ref=gm_prev.at[w], send_sem=s_gm.at[0, z, w],
+            recv_sem=s_edge_gm.at[0, w], device_id=beside(1, z), device_id_type=MESH)
+
+    def first_rows(z, w):
+        return pltpu.make_async_remote_copy(
+            src_ref=gm_slot.at[0, pl.ds(w * 32, EDGE), :], dst_ref=gm_next.at[w], send_sem=s_gm.at[1, z, w],
+            recv_sem=s_edge_gm.at[1, w], device_id=beside(-1, z), device_id_type=MESH)
+
+    @pl.when(zh == NZ - 1)
+    def _():
+        for z in range(NZ):
+            for w in range(2):
+                last_rows(z, w).start()
+
+    @pl.when(zh == 0)
+    def _():
+        for z in range(NZ):
+            for w in range(2):
+                first_rows(z, w).start()
+
+    for n, (dz, db) in enumerate(far):
+        arrived(x_slot(dz, db, 1 - core), s_x.at[10 + n], r_x.at[10 + n])
     for z in range(NZ):
         inv = inverse(z)
         values = jnp.concatenate([x_recv[z * NC + c].astype(F32) for c in range(NC)], axis=1)
         b_slot[z] = gelu_tanh(values * inv * gain_b_all).astype(BF)
     edges(b_slot, 32, b_prev, b_next, 2)
 
-    inner = in_send[...]
-    for d in (1, 2, 3):
-        at = (ch - d + NC) % NC
-        arrived(in_recv.at[at], s_col.at[3, d], r_col.at[3, d])
-        inner += in_recv[at]
-    inner = jnp.concatenate([inner * (1.0 / CMID)] * 4, axis=1)
-    grad_mid = (inv_b * (grad_n - normed_b * inner)).astype(BF)
-    gm_slot[zh] = dot(grad_mid, one_hot_rows(rows_ref[:, 3:4], 384)).astype(BF)
-    for d in (1, 2, 3):
-        start(gm_slot.at[zh], gm_slot.at[zh], s_col.at[4, d], r_col.at[4, d], at_z(d))
+    for d in (1, 2, 3):
+        arrived(gm_slot.at[slot_of(d)], s_col.at[4, d], r_col.at[4, d])
+
+    for w in range(2):
+        arrived(gm_prev.at[w], s_gm.at[0, 0, w], s_edge_gm.at[0, w])
+        arrived(gm_next.at[w], s_gm.at[1, 0, w], s_edge_gm.at[1, w])
+    lay(gm_slot, 32, gm_prev, gm_next, gm_rows)
+    before, here, after = shifted(gm_rows, 128)
+    back_conv(before, here, after, turned_a, 128, out_rows)
+    to_twin(out_rows, 64, out_over, out_twin, 1)
+    from_twin(out_rows, 64, out_twin, out_send, 1)
+    scatter(out_send, out_recv, s_o, r_o)
 
     edges_done(b_prev, b_next, 2)
     lay(b_slot, 32, b_prev, b_next, b_rows)
@@ -503,41 +623,19 @@
             pool_send[z, w * 16 : (w + 1) * 16, :] = total[w * 64 + z * 16 : w * 64 + (z + 1) * 16].astype(BF)
 
     for d in (1, 2, 3):
-        arrived(gm_slot.at[slot_of(d)], s_col.at[4, d], r_col.at[4, d])
-    edges(gm_slot, 32, gm_prev, gm_next, 3)
-    for d in (1, 2, 3):
         t = (zh + d) % NZ
         start(pool_send.at[t], pool_recv.at[zh], s_col.at[5, d], r_col.at[5, d], at_z(d))
 
-    edges_done(gm_prev, gm_next, 3)
-    lay(gm_slot, 32, gm_prev, gm_next, gm_rows)
-    before, here, after = shifted(gm_rows, 128)
-    back_conv(before, here, after, turned_a, 128, out_rows)
-    for z in range(NZ):
-        for c in range(NC):
-            for w in range(2):
-                out_send[z * NC + c, w * 64 : (w + 1) * 64, :] = out_rows[w, c, z * 64 : (z + 1) * 64, :].astype(BF)
-    scatter(out_send, out_recv, s_o, r_o, True)
-    out_recv[own] = out_send[own]
-
     for d in (1, 2, 3):
         arrived(pool_recv.at[slot_of(d)], s_col.at[5, d], r_col.at[5, d])
     total = jnp.concatenate([acc_b[w, pl.ds(pl.multiple_of(zh * 16, 16), 16), :] for w in range(2)], axis=0)
     for d in (1, 2, 3):
         total += pool_recv[slot_of(d)].astype(F32)
-    pooled_ref[...] = (total + bias_b_ref[...]).astype(BF)
+    pooled_ref[...] = (total + bias_b_ref[...].reshape(1, 384)).astype(BF).reshape(2, 16, 384)
 
     scattered(out_recv, s_o, r_o)
-    back = jnp.concatenate(
-        [
-            out_recv[z * NC].astype(F32) + out_recv[z * NC + 1].astype(F32)
-            + out_recv[z * NC + 2].astype(F32) + out_recv[z * NC + 3].astype(F32)
-            for z in range(NZ)
-        ],
-        axis=1,
-    )
-    grad_n = back * factor_a
-    ia_send[...] = jnp.broadcast_to(jnp.sum(grad_n * normed_a, axis=-1, keepdims=True), (128, 128))
+    grad_n = two_shares(out_recv) * factor_a
+    ia_send[...] = to_row(jnp.sum(grad_n * normed_a, axis=-1, keepdims=True))
     for d in (1, 2, 3):
         start(ia_send, ia_recv.at[ch], s_col.at[6, d], r_col.at[6, d], at_c(d))
     hot = one_hot_rows(rows_ref[:, 4:5], 384)
@@ -546,15 +644,26 @@
         at = (ch - d + NC) % NC
         arrived(ia_recv.at[at], s_col.at[6, d], r_col.at[6, d])
         inner += ia_recv[at]
-    inner = jnp.concatenate([inner * (1.0 / CIN)] * 4, axis=1)
+    inner = jnp.concatenate([to_column(inner * (1.0 / CIN), 128)] * 4, axis=1)
     grad = (inv_a * (grad_n - normed_a * inner)).astype(BF)
-    grad_ref[...] = dot(grad, hot)[:, 0:320].astype(BF)
+    grad_ref[...] = dot(grad, hot)[:, 0:320].astype(BF).reshape(2, 64, 320)
 
     for copy in pending:
         copy.wait_send()
     scatter_sent(back_send, s_b, r_b)
-    scatter_sent(x_send, s_x, r_x)
     scatter_sent(out_send, s_o, r_o)
+
+    @pl.when(zh == NZ - 1)
+    def _():
+        for z in range(NZ):
+            for w in range(2):
+                last_rows(z, w).wait_send()
+
+    @pl.when(zh == 0)
+    def _():
+        for z in range(NZ):
+            for w in range(2):
+                first_rows(z, w).wait_send()
 
 
 def per_device(dna_features, gain_a, conv_a, bias_a, gain_b, conv_b, bias_b, grad_out):
@@ -563,37 +672,40 @@
     vmem = pltpu.VMEM
     pooled, grad = pl.pallas_call(
         kernel,
-        out_shape=(jax.ShapeDtypeStruct((32, 384), BF), jax.ShapeDtypeStruct((128, 320), BF)),
-        in_specs=[pl.BlockSpec(memory_space=vmem)] * 10,
+        out_shape=(jax.ShapeDtypeStruct((2, 16, 384), BF), jax.ShapeDtypeStruct((2, 64, 320), BF)),
+        in_specs=[pl.BlockSpec(memory_space=pl.ANY)] * 10,
         out_specs=[pl.BlockSpec(memory_space=vmem)] * 2,
         scratch_shapes=[
+            vmem((2, 64, CIN), BF), vmem((5, 10, 352), BF), vmem((5, 11, 384), BF), vmem((CIN,), F32), vmem((352,), F32),
+            vmem((CMID,), F32), vmem((384,), F32), vmem((2, 16, 384), BF), vmem((8, 1536), jnp.int32), vmem((512, 8), jnp.int32),
             vmem((8, 64, 384), BF), vmem((4, 64, 384), BF), vmem((512, WIDE), BF), vmem((512, WIDE), BF),
             vmem((512, WIDE), BF), vmem((8, 384), F32),
             vmem((4, 128, 384), BF), vmem((2, 16, 384), BF), vmem((2, 16, 384), BF), vmem((2, 3, 288, 128), F32),
-            vmem((5, 256, 512), BF), vmem((4, 128, 384), BF),
-            vmem((4, 32, 384), BF), vmem((2, 16, 384), BF), vmem((2, 16, 384), BF), vmem((2, 3, 96, 128), F32),
-            vmem((2, 4, 128, 128), F32), vmem((16, 64, 128), BF), vmem((16, 64, 128), BF),
-            vmem((2, 128, 384), F32), vmem((4, 64, 384), BF), vmem((4, 64, 384), BF),
+            vmem((5, 256, 512), BF), vmem((4, 64, 384), BF),
+            vmem((4, 32, 384), BF), vmem((32, 384), BF), vmem((2, 16, 384), BF), vmem((2, 16, 384), BF), vmem((2, 3, 96, 128), F32),
+            vmem((2, 4, 128, 128), F32), vmem((8, 64, 128), BF), vmem((8, 64, 128), BF), vmem((8, 64, 128), BF),
+            vmem((8, 64, 128), BF), vmem((2, 128, 384), F32), vmem((4, 64, 384), BF), vmem((4, 64, 384), BF),
             vmem((4, 64, 128), BF), vmem((16, 64, 128), BF), vmem((4, 64, 512), BF), vmem((2, 16, 512), BF),
             vmem((2, 16, 512), BF), vmem((2, 4, 160, 128), F32),
             vmem((4, 32, 384), BF), vmem((4, 32, 384), BF), vmem((2, 64, 384), F32),
-            vmem((64, 128), F32), vmem((4, 64, 128), F32), vmem((4, 64, 384), BF), vmem((2, 16, 384), BF),
+            vmem((8, 128), F32), vmem((4, 8, 128), F32), vmem((4, 64, 384), BF), vmem((2, 16, 384), BF),
             vmem((2, 16, 384), BF), vmem((2, 3, 160, 128), F32),
-            vmem((2, 4, 256, 128), F32), vmem((16, 128, 128), BF), vmem((16, 128, 128), BF),
-            vmem((128, 128), F32), vmem((4, 128, 128), F32),
-            dma((2, 4)), dma((2, 4)), dma((4,)), dma((4,)), dma((2, 4)), dma((2, 4)), dma((2, 2)), dma((2, 2)),
+            vmem((2, 4, 256, 128), F32), vmem((8, 128, 128), BF), vmem((8, 128, 128), BF), vmem((8, 128, 128), BF),
+            vmem((8, 128, 128), BF),
+            vmem((8, 128), F32), vmem((4, 8, 128), F32),
+            dma((2, 4)), dma((2, 4)), dma((4,)), dma((4,)), dma((2, 4, 2)), dma((2, 4, 2)), dma((2, 2, 2)), dma((2, 2, 2)),
             dma((7, 4)), dma((7, 4)), dma((4, 4)), dma((4, 4)),
-            dma((16,)), dma((16,)), dma((16,)), dma((16,)), dma((16,)), dma((16,)),
+            dma((16,)), dma((16,)), dma((16,)), dma((16,)), dma((16,)), dma((16,)), dma((10,)), dma((2, 4, 2)), dma((2, 2)), dma((4,)), dma((4,)),
+            dma((2,)), dma((2,)),
         ],
         compiler_params=pltpu.CompilerParams(
-            collective_id=0, has_side_effects=True, vmem_limit_bytes=48 * 1024 * 1024
+            collective_id=0, has_side_effects=True, vmem_limit_bytes=60 * 1024 * 1024
         ),
         cost_estimate=pl.CostEstimate(flops=3_000_000_000, bytes_accessed=8_000_000, transcendentals=800_000),
     )(
-        dna_features.reshape(128, CIN), conv_a, conv_b, gain_a.reshape(1, CIN), bias_a.reshape(1, 352),
-        gain_b.reshape(1, CMID), bias_b.reshape(1, 384), grad_out.reshape(32, 384), jnp.asarray(lanes), jnp.asarray(rows),
+        dna_features, conv_a, conv_b, gain_a, bias_a, gain_b, bias_b, grad_out, jnp.asarray(lanes), jnp.asarray(rows),
     )
-    return pooled.reshape(2, 16, 384), grad.reshape(2, 64, 320)
+    return pooled, grad
 
 
 def solution(mesh):

time: 109 us -> 95.3 us (0.87)
  Pallas kernels: 99.3 us -> 91.5 us
  local copies, waits for them, and re-layouts: 8.4 us -> 2.89 us
    pallas_call x1, Pallas kernels: 99.3 us -> 91.5 us  [per_device(): pl.pallas_call(kernel, out_shape=(jax.ShapeDtypeStruct((2, 16, 384), BF),...]
    reshape x4 -> x0, local copies, waits for them, and re-layouts: 2.77 us -> none  [the longest x1 0.7 us: per_device(): gain_b.reshape(1, CMID)]
    unnamed x14 -> x2, local copies, waits for them, and re-layouts: 5.63 us -> 2.89 us
where the time goes in v2:
time: 95.3 us; the launch traced here: 95 us
  Pallas kernels  91.5 us (96%)
  local copies, waits for them, and re-layouts  2.89 us (3%)
    pallas_call x1, Pallas kernels, per_device(): pl.pallas_call(kernel, out_shape=(jax.ShapeDtypeStruct((2, 16, 384), BF),...  91.5 us
    unnamed x2, local copies, waits for them, and re-layouts  2.89 us

profile of v2, /device:TPU:1, one launch (start us, length us, event | category | flops | bytes accessed | tf_op | source)
XLA Modules:
  0.0 95.0 jit_solution(14816614292205105549)
XLA Ops:
  0.6 91.5 %shard_map.113 = (bf16[2,16,384]{2,1,0:T(8,128)(2,1)}, bf16[2,64,320]{2,1,0:T(8,128)(2,1)}) custom-call(bf16[2,64,1280]{2,1,0:T(8,128)(2,1)} %feat_in.1, bf16[5,10,352]{2,1,0:T(8,128)(2,1)} %wa_in.1, bf16[5,11,384]{2,1,0:T(8,128)(2,1)} %wb_in.1, f32[1280]{0:T(1024)} %gain_a_in.1, f32[352]{0:T(512)} %bias_a_in.1, f32[1408]{0:T(1024)} %gain_b_in.1, ...), custom_call_target="tpu_custom_call" | custom-call | flops 3000000000 | bytes 8000000 | tf_op jit(solution)/shard_map/pallas_call | solution.py:673
  92.1 1.3 %copy.14 = bf16[2,16,384]{2,1,0:T(8,128)(2,1)} copy(bf16[2,16,384]{2,1,0:T(8,128)(2,1)} %get-tuple-element.4) | data formatting | bytes 49152
  93.5 1.5 %copy.15 = bf16[2,64,320]{2,1,0:T(8,128)(2,1)} copy(bf16[2,64,320]{2,1,0:T(8,128)(2,1)} %get-tuple-element.5) | data formatting | bytes 163840

commit v3 on v2

--- a/solution.py
+++ b/solution.py
@@ -182,6 +182,7 @@
         greet(at_x(d))
     for d in (-1, 1):
         greet(at_y(d))
+        greet(at_y(2 * d))
         for z in range(NZ):
             greet(beside(d, z))
 
@@ -212,23 +213,27 @@
     for c in range(NC):
         whole_b[c * 128 + 96 : c * 128 + 128, 0:TAPS] = jnp.zeros((32, TAPS), BF)
     taps_a[:, :, 384:512] = jnp.zeros((5, 256, 128), BF)
-    pl.semaphore_wait(barrier, 28)
-
-    half = ((0, 32), (32, 32))
+    pl.semaphore_wait(barrier, 30)
+
     parts = ((0, 1152), (1152, 768))
 
-    def ring_fa(r, way):
-        sign = 1 if way == 0 else -1
-        at, n = (0, 64) if r < 3 else half[way]
-        b = (yi - sign * r + NY) % NY
-        ref = first_a.at[b, pl.ds(at, n), :]
-        start(ref, ref, s_fa.at[way, r], r_fa.at[way, r], at_y(sign))
-
-    def ring_fa_done(r, way):
-        sign = 1 if way == 0 else -1
-        at, n = (0, 64) if r < 3 else half[way]
-        b = (yi - sign * (r + 1) + NY) % NY
-        arrived(first_a.at[b, pl.ds(at, n), :], s_fa.at[way, r], r_fa.at[way, r])
+    def first_block(d, at=0, n=64):
+        return first_a.at[(yi + d + NY) % NY, pl.ds(at, n), :]
+
+    hops = (
+        ((0, 1, 0, 64), (0, -1, 0, 64), (0, 2, 0, 64), (0, -2, 0, 64)),
+        ((-2, 1, 0, 64), (2, -1, 0, 64), (-2, 2, 0, 32), (2, -2, 32, 32)),
+    )
+
+    def send_first(step):
+        for n, (b, to, at, rows) in enumerate(hops[step]):
+            ref = first_block(b, at, rows)
+            start(ref, ref, s_fa.at[step, n], r_fa.at[step, n], at_y(to))
+
+    def first_done(step, which):
+        for n in which:
+            b, to, at, rows = hops[step][n]
+            arrived(first_block(b - to, at, rows), s_fa.at[step, n], r_fa.at[step, n])
 
     def place_a(b):
         return pl.multiple_of(b * 80, 16)
@@ -263,8 +268,7 @@
             if r + 1 < last or (r + 1 == last and rank == 0):
                 ring(r + 1, way, c)
 
-    for way in (0, 1):
-        ring_fa(0, way)
+    send_first(0)
     for d in (1, 2, 3):
         start(first_b.at[xi], first_b.at[xi], s_fb.at[d], r_fb.at[d], at_x(d))
 
@@ -294,12 +298,8 @@
         ref = act_slot.at[slot_of(d), mine, :]
         start(ref, ref, s_af.at[d], r_af.at[d], twin)
 
-    def fa_on(r):
-        for way in (0, 1):
-            ring_fa_done(r, way)
-            ring_fa(r + 1, way)
-
     subset(2)
+    subset(1)
 
     for d in (1, 2, 3):
         arrived(first_b.at[(xi - d + NX) % NX], s_fb.at[d], r_fb.at[d])
@@ -310,11 +310,9 @@
     for rank in (0, 1):
         for way in (0, 1):
             ring_wb(0, way, way if rank == 0 else 1 - way)
-    fa_on(0)
-    subset(1)
-    fa_on(1)
+    first_done(0, (2, 3))
+    send_first(1)
     subset(3)
-    fa_on(2)
     subset(0)
     g_own = g_ref[...].reshape(32, 384)
     g_slot[zh] = g_own
@@ -322,8 +320,8 @@
     for d in (1, 2, 3):
         start(g_send, g_slot.at[zh], s_col.at[0, d], r_col.at[0, d], at_z(d))
     hot_a = one_hot_rows(rows_ref[0:400, 1:2], 512)
-    for way in (0, 1):
-        ring_fa_done(3, way)
+    first_done(0, (0, 1))
+    first_done(1, range(4))
     block = dot(hot_a, first_a[...].reshape(512, 384)).astype(BF)
     for k in range(5):
         whole_a[pl.ds(place_a(xi), 80), k * 384 : (k + 1) * 384] = block[k * 80 : (k + 1) * 80]
@@ -397,13 +395,8 @@
                 where[w, t, pl.ds(0, rows, stride=2), :] = even[w * rows : (w + 1) * rows, lanes]
                 where[w, t, pl.ds(1, rows, stride=2), :] = odd[w * rows : (w + 1) * rows, lanes]
 
-    gain_b = jnp.concatenate([gain_b, jnp.zeros((1, 128), F32)], axis=1)
-    hot = one_hot_lanes(lanes_ref[2:3, 0:512] + zh * 11, CMID + 128)
-    gain_b_all = spread_gain(gain_b, hot)
     pass_on(ring_wb, ring_wb_done, 1, 3, 0)
     pass_on(ring_wa, ring_wa_done, 0, 1, 0)
-    hot = one_hot_lanes(lanes_ref[1:2, 0:512] + ch * 352, CMID + 128)
-    gain_b_own = spread_gain(gain_b, hot)
     for d in (1, 2, 3):
         arrived(g_slot.at[slot_of(d)], s_col.at[0, d], r_col.at[0, d])
     edges(g_slot, 16, g_prev, g_next, 0)
@@ -411,14 +404,7 @@
     for d in range(NZ):
         arrived(act_slot.at[slot_of(d), others, :], s_af.at[d], r_af.at[d])
     edges(act_slot, 64, act_prev, act_next, 1)
-    hot = one_hot_lanes(lanes_ref[3:4, 0:512] + ch * 320, CIN)
-    gain_a_own = spread_gain(gain_a, hot)
-    feat_bf = feat_ref[...].reshape(128, CIN)
-    inv_a = inverse_a(feat_bf.astype(F32))
-    feat_own = dot(feat_bf, hot)
     pass_on(ring_wb, ring_wb_done, 2, 3, 0)
-    normed_a = feat_own * inv_a
-    factor_a = gelu_slope(normed_a * gain_a_own) * gain_a_own
     edges_done(g_prev, g_next, 0)
     lay(g_slot, 16, g_prev, g_next, g_rows)
     edges_done(act_prev, act_next, 1)
@@ -504,6 +490,10 @@
     from_twin(back_rows, 32, back_twin, back_send, 0)
     scatter(back_send, back_recv, s_b, r_b)
 
+    gain_b = jnp.concatenate([gain_b, jnp.zeros((1, 128), F32)], axis=1)
+    hot = one_hot_lanes(lanes_ref[1:2, 0:512] + ch * 352, CMID + 128)
+    gain_b_own = spread_gain(gain_b, hot)
+
     for d in (1, 2, 3):
         arrived(mid_recv.at[slot_of(d)], s_col.at[2, d], r_col.at[2, d])
     total = jnp.concatenate([acc_a[w, pl.ds(pl.multiple_of(zh * 32, 32), 32), :] for w in range(2)], axis=0)
@@ -531,6 +521,9 @@
     def x_slot(dz, db, side):
         return x_recv.at[slot_of(dz) * NC + ((zl - db + 2) % 2) * 2 + side]
 
+    hot = one_hot_lanes(lanes_ref[2:3, 0:512] + zh * 11, CMID + 128)
+    gain_b_all = spread_gain(gain_b, hot)
+
     hot = one_hot_rows(rows_ref[:, 0:1], 512)
     for k in range(4):
         turned_a[:, k * 512 : (k + 1) * 512] = dot(hot, whole_a[:, k * 512 : (k + 1) * 512]).astype(BF)
@@ -589,6 +582,14 @@
             for w in range(2):
                 first_rows(z, w).start()
 
+    hot = one_hot_lanes(lanes_ref[3:4, 0:512] + ch * 320, CIN)
+    gain_a_own = spread_gain(gain_a, hot)
+    feat_bf = feat_ref[...].reshape(128, CIN)
+    inv_a = inverse_a(feat_bf.astype(F32))
+    feat_own = dot(feat_bf, hot)
+    normed_a = feat_own * inv_a
+    factor_a = gelu_slope(normed_a * gain_a_own) * gain_a_own
+
     for n, (dz, db) in enumerate(far):
         arrived(x_slot(dz, db, 1 - core), s_x.at[10 + n], r_x.at[10 + n])
     for z in range(NZ):
@@ -607,9 +608,6 @@
     before, here, after = shifted(gm_rows, 128)
     back_conv(before, here, after, turned_a, 128, out_rows)
     to_twin(out_rows, 64, out_over, out_twin, 1)
-    from_twin(out_rows, 64, out_twin, out_send, 1)
-    scatter(out_send, out_recv, s_o, r_o)
-
     edges_done(b_prev, b_next, 2)
     lay(b_slot, 32, b_prev, b_next, b_rows)
     taps = pooled_taps(b_rows, 64)
@@ -621,6 +619,9 @@
     for z in range(NZ):
         for w in range(2):
             pool_send[z, w * 16 : (w + 1) * 16, :] = total[w * 64 + z * 16 : w * 64 + (z + 1) * 16].astype(BF)
+
+    from_twin(out_rows, 64, out_twin, out_send, 1)
+    scatter(out_send, out_recv, s_o, r_o)
 
     for d in (1, 2, 3):
         t = (zh + d) % NZ

time: 95.3 us -> 88.3 us (0.927)
  Pallas kernels: 91.5 us -> 84.5 us
    pallas_call x1, Pallas kernels: 91.5 us -> 84.5 us  [per_device(): pl.pallas_call(kernel, out_shape=(jax.ShapeDtypeStruct((2, 16, 384), BF),...]
where the time goes in v3:
time: 88.3 us; the launch traced here: 88.1 us
  Pallas kernels  84.5 us (96%)
  local copies, waits for them, and re-layouts  2.89 us (3%)
    pallas_call x1, Pallas kernels, per_device(): pl.pallas_call(kernel, out_shape=(jax.ShapeDtypeStruct((2, 16, 384), BF),...  84.5 us
    unnamed x2, local copies, waits for them, and re-layouts  2.89 us

profile of v3, /device:TPU:1, one launch (start us, length us, event | category | flops | bytes accessed | tf_op | source)
XLA Modules:
  0.0 88.1 jit_solution(5896603601076556838)
XLA Ops:
  0.6 84.5 %shard_map.113 = (bf16[2,16,384]{2,1,0:T(8,128)(2,1)}, bf16[2,64,320]{2,1,0:T(8,128)(2,1)}) custom-call(bf16[2,64,1280]{2,1,0:T(8,128)(2,1)} %feat_in.1, bf16[5,10,352]{2,1,0:T(8,128)(2,1)} %wa_in.1, bf16[5,11,384]{2,1,0:T(8,128)(2,1)} %wb_in.1, f32[1280]{0:T(1024)} %gain_a_in.1, f32[352]{0:T(512)} %bias_a_in.1, f32[1408]{0:T(1024)} %gain_b_in.1, ...), custom_call_target="tpu_custom_call" | custom-call | flops 3000000000 | bytes 8000000 | tf_op jit(solution)/shard_map/pallas_call | solution.py:674
  85.2 1.3 %copy.14 = bf16[2,16,384]{2,1,0:T(8,128)(2,1)} copy(bf16[2,16,384]{2,1,0:T(8,128)(2,1)} %get-tuple-element.4) | data formatting | bytes 49152
  86.5 1.5 %copy.15 = bf16[2,64,320]{2,1,0:T(8,128)(2,1)} copy(bf16[2,64,320]{2,1,0:T(8,128)(2,1)} %get-tuple-element.5) | data formatting | bytes 163840

commit v4 on v3

--- a/solution.py
+++ b/solution.py
@@ -319,6 +319,7 @@
     g_send[...] = g_own
     for d in (1, 2, 3):
         start(g_send, g_slot.at[zh], s_col.at[0, d], r_col.at[0, d], at_z(d))
+    pass_on(ring_wb, ring_wb_done, 0, 3, 0)
     hot_a = one_hot_rows(rows_ref[0:400, 1:2], 512)
     first_done(0, (0, 1))
     first_done(1, range(4))
@@ -328,7 +329,6 @@
     for rank in (0, 1):
         for way in (0, 1):
             ring_wa(0, way, way if rank == 0 else 1 - way)
-    pass_on(ring_wb, ring_wb_done, 0, 3, 0)
     for d in (1, 3, 2):
         arrived(act_slot.at[slot_of(d), mine, :], s_col.at[1, d], r_col.at[1, d])
         share_act(d)

time: 88.3 us -> 90 us (1.019)
  Pallas kernels: 84.5 us -> 86.3 us
    pallas_call x1, Pallas kernels: 84.5 us -> 86.3 us  [per_device(): pl.pallas_call(kernel, out_shape=(jax.ShapeDtypeStruct((2, 16, 384), BF),...]
where the time goes in v4:
time: 90 us; the launch traced here: 89.8 us
  Pallas kernels  86.3 us (96%)
  local copies, waits for them, and re-layouts  2.89 us (3%)
    pallas_call x1, Pallas kernels, per_device(): pl.pallas_call(kernel, out_shape=(jax.ShapeDtypeStruct((2, 16, 384), BF),...  86.3 us
    unnamed x2, local copies, waits for them, and re-layouts  2.89 us

profile of v4, /device:TPU:1, one launch (start us, length us, event | category | flops | bytes accessed | tf_op | source)
XLA Modules:
  0.0 89.8 jit_solution(7919237793554609390)
XLA Ops:
  0.6 86.3 %shard_map.113 = (bf16[2,16,384]{2,1,0:T(8,128)(2,1)}, bf16[2,64,320]{2,1,0:T(8,128)(2,1)}) custom-call(bf16[2,64,1280]{2,1,0:T(8,128)(2,1)} %feat_in.1, bf16[5,10,352]{2,1,0:T(8,128)(2,1)} %wa_in.1, bf16[5,11,384]{2,1,0:T(8,128)(2,1)} %wb_in.1, f32[1280]{0:T(1024)} %gain_a_in.1, f32[352]{0:T(512)} %bias_a_in.1, f32[1408]{0:T(1024)} %gain_b_in.1, ...), custom_call_target="tpu_custom_call" | custom-call | flops 3000000000 | bytes 8000000 | tf_op jit(solution)/shard_map/pallas_call | solution.py:674
  86.9 1.3 %copy.14 = bf16[2,16,384]{2,1,0:T(8,128)(2,1)} copy(bf16[2,16,384]{2,1,0:T(8,128)(2,1)} %get-tuple-element.4) | data formatting | bytes 49152
  88.2 1.5 %copy.15 = bf16[2,64,320]{2,1,0:T(8,128)(2,1)} copy(bf16[2,64,320]{2,1,0:T(8,128)(2,1)} %get-tuple-element.5) | data formatting | bytes 163840

commit v5 on v3

--- a/solution.py
+++ b/solution.py
@@ -299,7 +299,8 @@
         start(ref, ref, s_af.at[d], r_af.at[d], twin)
 
     subset(2)
-    subset(1)
+    first_done(0, (2, 3))
+    send_first(1)
 
     for d in (1, 2, 3):
         arrived(first_b.at[(xi - d + NX) % NX], s_fb.at[d], r_fb.at[d])
@@ -310,8 +311,7 @@
     for rank in (0, 1):
         for way in (0, 1):
             ring_wb(0, way, way if rank == 0 else 1 - way)
-    first_done(0, (2, 3))
-    send_first(1)
+    subset(1)
     subset(3)
     subset(0)
     g_own = g_ref[...].reshape(32, 384)

time: 88.3 us -> 86.6 us (0.981)
  Pallas kernels: 84.5 us -> 82.8 us
    pallas_call x1, Pallas kernels: 84.5 us -> 82.8 us  [per_device(): pl.pallas_call(kernel, out_shape=(jax.ShapeDtypeStruct((2, 16, 384), BF),...]
where the time goes in v5:
time: 86.6 us; the launch traced here: 86.4 us
  Pallas kernels  82.8 us (96%)
  local copies, waits for them, and re-layouts  2.89 us (3%)
    pallas_call x1, Pallas kernels, per_device(): pl.pallas_call(kernel, out_shape=(jax.ShapeDtypeStruct((2, 16, 384), BF),...  82.8 us
    unnamed x2, local copies, waits for them, and re-layouts  2.89 us

profile of v5, /device:TPU:1, one launch (start us, length us, event | category | flops | bytes accessed | tf_op | source)
XLA Modules:
  0.0 86.4 jit_solution(6127334345791901651)
XLA Ops:
  0.6 82.8 %shard_map.113 = (bf16[2,16,384]{2,1,0:T(8,128)(2,1)}, bf16[2,64,320]{2,1,0:T(8,128)(2,1)}) custom-call(bf16[2,64,1280]{2,1,0:T(8,128)(2,1)} %feat_in.1, bf16[5,10,352]{2,1,0:T(8,128)(2,1)} %wa_in.1, bf16[5,11,384]{2,1,0:T(8,128)(2,1)} %wb_in.1, f32[1280]{0:T(1024)} %gain_a_in.1, f32[352]{0:T(512)} %bias_a_in.1, f32[1408]{0:T(1024)} %gain_b_in.1, ...), custom_call_target="tpu_custom_call" | custom-call | flops 3000000000 | bytes 8000000 | tf_op jit(solution)/shard_map/pallas_call | solution.py:674
  83.5 1.3 %copy.14 = bf16[2,16,384]{2,1,0:T(8,128)(2,1)} copy(bf16[2,16,384]{2,1,0:T(8,128)(2,1)} %get-tuple-element.4) | data formatting | bytes 49152
  84.8 1.5 %copy.15 = bf16[2,64,320]{2,1,0:T(8,128)(2,1)} copy(bf16[2,64,320]{2,1,0:T(8,128)(2,1)} %get-tuple-element.5) | data formatting | bytes 163840

commit v6 on v5

--- a/solution.py
+++ b/solution.py
@@ -611,6 +611,9 @@
     edges_done(b_prev, b_next, 2)
     lay(b_slot, 32, b_prev, b_next, b_rows)
     taps = pooled_taps(b_rows, 64)
+    from_twin(out_rows, 64, out_twin, out_send, 1)
+    scatter(out_send, out_recv, s_o, r_o)
+
     total = dot(taps[0], whole_b[:, 0:384])
     for k in range(1, 5):
         total += dot(taps[k], whole_b[:, k * 384 : (k + 1) * 384])
@@ -620,8 +623,6 @@
         for w in range(2):
             pool_send[z, w * 16 : (w + 1) * 16, :] = total[w * 64 + z * 16 : w * 64 + (z + 1) * 16].astype(BF)
 
-    from_twin(out_rows, 64, out_twin, out_send, 1)
-    scatter(out_send, out_recv, s_o, r_o)
 
     for d in (1, 2, 3):
         t = (zh + d) % NZ

time: 86.6 us -> 86.4 us (level)
  no operation moved by 1% of the time
where the time goes in v6:
time: 86.4 us; the launch traced here: 86.2 us
  Pallas kernels  82.6 us (96%)
  local copies, waits for them, and re-layouts  2.89 us (3%)
    pallas_call x1, Pallas kernels, per_device(): pl.pallas_call(kernel, out_shape=(jax.ShapeDtypeStruct((2, 16, 384), BF),...  82.6 us
    unnamed x2, local copies, waits for them, and re-layouts  2.89 us

profile of v6, /device:TPU:1, one launch (start us, length us, event | category | flops | bytes accessed | tf_op | source)
XLA Modules:
  0.0 86.2 jit_solution(6763809393614714201)
XLA Ops:
  0.6 82.6 %shard_map.113 = (bf16[2,16,384]{2,1,0:T(8,128)(2,1)}, bf16[2,64,320]{2,1,0:T(8,128)(2,1)}) custom-call(bf16[2,64,1280]{2,1,0:T(8,128)(2,1)} %feat_in.1, bf16[5,10,352]{2,1,0:T(8,128)(2,1)} %wa_in.1, bf16[5,11,384]{2,1,0:T(8,128)(2,1)} %wb_in.1, f32[1280]{0:T(1024)} %gain_a_in.1, f32[352]{0:T(512)} %bias_a_in.1, f32[1408]{0:T(1024)} %gain_b_in.1, ...), custom_call_target="tpu_custom_call" | custom-call | flops 3000000000 | bytes 8000000 | tf_op jit(solution)/shard_map/pallas_call | solution.py:675
  83.3 1.3 %copy.14 = bf16[2,16,384]{2,1,0:T(8,128)(2,1)} copy(bf16[2,16,384]{2,1,0:T(8,128)(2,1)} %get-tuple-element.4) | data formatting | bytes 49152
  84.6 1.5 %copy.15 = bf16[2,64,320]{2,1,0:T(8,128)(2,1)} copy(bf16[2,64,320]{2,1,0:T(8,128)(2,1)} %get-tuple-element.5) | data formatting | bytes 163840

commit v7 on v5

--- a/solution.py
+++ b/solution.py
@@ -395,8 +395,8 @@
                 where[w, t, pl.ds(0, rows, stride=2), :] = even[w * rows : (w + 1) * rows, lanes]
                 where[w, t, pl.ds(1, rows, stride=2), :] = odd[w * rows : (w + 1) * rows, lanes]
 
+    pass_on(ring_wa, ring_wa_done, 0, 1, 0)
     pass_on(ring_wb, ring_wb_done, 1, 3, 0)
-    pass_on(ring_wa, ring_wa_done, 0, 1, 0)
     for d in (1, 2, 3):
         arrived(g_slot.at[slot_of(d)], s_col.at[0, d], r_col.at[0, d])
     edges(g_slot, 16, g_prev, g_next, 0)

time: 86.6 us -> 87.1 us (level)
  no operation moved by 1% of the time
where the time goes in v7:
time: 87.1 us; the launch traced here: 86.3 us
  Pallas kernels  82.8 us (95%)
  local copies, waits for them, and re-layouts  2.89 us (3%)
    pallas_call x1, Pallas kernels, per_device(): pl.pallas_call(kernel, out_shape=(jax.ShapeDtypeStruct((2, 16, 384), BF),...  82.8 us
    unnamed x2, local copies, waits for them, and re-layouts  2.89 us

profile of v7, /device:TPU:1, one launch (start us, length us, event | category | flops | bytes accessed | tf_op | source)
XLA Modules:
  0.0 86.3 jit_solution(6570398600584665186)
XLA Ops:
  0.6 82.8 %shard_map.113 = (bf16[2,16,384]{2,1,0:T(8,128)(2,1)}, bf16[2,64,320]{2,1,0:T(8,128)(2,1)}) custom-call(bf16[2,64,1280]{2,1,0:T(8,128)(2,1)} %feat_in.1, bf16[5,10,352]{2,1,0:T(8,128)(2,1)} %wa_in.1, bf16[5,11,384]{2,1,0:T(8,128)(2,1)} %wb_in.1, f32[1280]{0:T(1024)} %gain_a_in.1, f32[352]{0:T(512)} %bias_a_in.1, f32[1408]{0:T(1024)} %gain_b_in.1, ...), custom_call_target="tpu_custom_call" | custom-call | flops 3000000000 | bytes 8000000 | tf_op jit(solution)/shard_map/pallas_call | solution.py:674
  83.4 1.3 %copy.14 = bf16[2,16,384]{2,1,0:T(8,128)(2,1)} copy(bf16[2,16,384]{2,1,0:T(8,128)(2,1)} %get-tuple-element.4) | data formatting | bytes 49152
  84.7 1.5 %copy.15 = bf16[2,64,320]{2,1,0:T(8,128)(2,1)} copy(bf16[2,64,320]{2,1,0:T(8,128)(2,1)} %get-tuple-element.5) | data formatting | bytes 163840
